TPU v7x, 128 devices: a whole 4x4x4 slice. The times are simulated.
128 devices in a mesh: seq: 64 (over y, z_lo, x, core), head: 2 (over z_hi).
Axes of the slice: x: 4, y: 4, z: 4 (z_hi: 2, z_lo: 2; z = z_hi * 2 + z_lo), core: 2. Of those that a mesh axis runs over, the one named last changes fastest.
Arguments:
- tokens: bfloat16 [57344, 1024], P('seq'), may hold values from -16 to 16
- log_decay: float32 [57344, 4], P('seq', 'head'), may hold values from -1 to 0
- starts: int32 [3], replicated, may hold values from 0 to 43008, as said below
- norm1_gain: float32 [1024], replicated, may hold values from 0.1 to 1.9
- norm1_bias: float32 [1024], replicated, may hold values from -1.75 to 1.75
- query_weight: bfloat16 [1024, 1024], P(None, 'head'), may hold values from -0.1875 to 0.1875
- key_weight: bfloat16 [1024, 1024], P(None, 'head'), may hold values from -0.1875 to 0.1875
- value_weight: bfloat16 [1024, 1728], P(None, 'head'), may hold values from -0.1875 to 0.1875
- gate_weight: bfloat16 [1024, 1728], P(None, 'head'), may hold values from -0.1875 to 0.1875
- output_weight: bfloat16 [1728, 1024], P('head'), may hold values from -0.25 to 0.25
- norm2_gain: float32 [1024], replicated, may hold values from 0.1 to 1.9
- norm2_bias: float32 [1024], replicated, may hold values from -1.75 to 1.75
- ffn_gate: bfloat16 [1024, 1728], P(None, 'head'), may hold values from -0.1875 to 0.1875
- ffn_up: bfloat16 [1024, 1728], P(None, 'head'), may hold values from -0.1875 to 0.1875
- ffn_down: bfloat16 [1728, 1024], P('head'), may hold values from -0.21875 to 0.21875
- cotangent: bfloat16 [57344, 1024], P('seq', 'head'), may hold values from -16 to 16
Outputs:
- output: bfloat16 [57344, 1024], P('seq', 'head')
- input_grad: bfloat16 [57344, 1024], P('seq', 'head')
- norm1_gain_grad: float32 [1024], P('seq')
- norm1_bias_grad: float32 [1024], P('seq')
- query_weight_grad: float32 [1024, 1024], P('seq', 'head')
- key_weight_grad: float32 [1024, 1024], P('seq', 'head')
- value_weight_grad: float32 [1024, 1728], P('seq', 'head')
- gate_weight_grad: float32 [1024, 1728], P('seq', 'head')
- output_weight_grad: float32 [1728, 1024], P('head', 'seq')
- norm2_gain_grad: float32 [1024], P('seq')
- norm2_bias_grad: float32 [1024], P('seq')
- ffn_gate_grad: float32 [1024, 1728], P('seq', 'head')
- ffn_up_grad: float32 [1024, 1728], P('seq', 'head')
- ffn_down_grad: float32 [1728, 1024], P('head', 'seq')
Inputs may be any that keep to these rules, and one draw needn't show every extreme that they name: starts[0] = 0 and the offsets rise strictly; every document has 14336 tokens or more; the last document starts at 43008.
All inputs are finite; a program needn't handle non-finite values.
Results may differ from a plain program's by a relative error of at most 0.035.
Values may be sent and summed in bfloat16 or wider, within the bound.
No kernel may reach another device: no remote copies, remote signals or barrier semaphores. Data moves between devices by JAX's collectives and lax.ppermute only.
A program may use at most 256 MiB of HBM per device.

v0:
```python
import math

import jax
import jax.numpy as jnp
from jax import lax
from jax.sharding import PartitionSpec as P

eps_norm = 1e-05
maximal_precision = lax.Precision.HIGHEST


def prefix(shard, axis, combine, identity, reverse):
    length, here = (lax.axis_size(axis), lax.axis_index(axis))
    everything = jax.tree.map(
        lambda part, kind: lax.all_gather(part.astype(kind), axis),
        shard,
        (jnp.bfloat16, jnp.bfloat16),
    )
    start = jax.tree.map(
        lambda part, zero: jnp.broadcast_to(jnp.asarray(zero, part.dtype), part.shape),
        shard,
        identity,
    )

    def step(k, before):
        at = length - 1 - k if reverse else k
        reached = at > here if reverse else at < here
        new = combine(
            before, jax.tree.map(lambda part, own: part[at].astype(own.dtype), everything, shard)
        )
        return jax.tree.map(lambda a, b: jnp.where(reached, a, b), new, before)

    return lax.fori_loop(0, length, step, start)


def layer_norm(values, gain_vec, bias_vec):
    average = jnp.mean(values, axis=-1, keepdims=True)
    centred = values - average
    variance = jnp.mean(centred * centred, axis=-1, keepdims=True)
    return centred * lax.rsqrt(variance + eps_norm) * gain_vec + bias_vec


def group_norm(values):
    average = jnp.mean(values, axis=-1, keepdims=True)
    centred = values - average
    variance = jnp.mean(centred * centred, axis=-1, keepdims=True)
    return centred * lax.rsqrt(variance + eps_norm)


def rotary_angles(positions, key_size):
    half_size = key_size // 2
    frequency = jnp.exp(-math.log(10000.0) * jnp.arange(half_size, dtype=jnp.float32) / half_size)
    return positions.astype(jnp.float32)[:, None] * frequency[None, :]


def rotate(vectors, angles):
    half_size = vectors.shape[-1] // 2
    upper_half = vectors[..., :half_size]
    lower_half = vectors[..., half_size:]
    cosine = jnp.cos(angles)[:, None, :]
    sine_part = jnp.sin(angles)[:, None, :]
    return jnp.concatenate(
        [
            upper_half * cosine - lower_half * sine_part,
            lower_half * cosine + upper_half * sine_part,
        ],
        axis=-1,
    )


def rotate_back(gradient, angles):
    half_size = gradient.shape[-1] // 2
    upper_half = gradient[..., :half_size]
    lower_half = gradient[..., half_size:]
    cosine = jnp.cos(angles)[:, None, :]
    sine_part = jnp.sin(angles)[:, None, :]
    return jnp.concatenate(
        [
            upper_half * cosine + lower_half * sine_part,
            lower_half * cosine - upper_half * sine_part,
        ],
        axis=-1,
    )


def links(starts, positions, block_start):
    started = starts[None, :] <= positions[:, None]
    doc_ids = jnp.sum(started.astype(jnp.int32), axis=1)
    inside = jnp.logical_and(starts[None, :] >= block_start, started)
    opened = jnp.sum(inside.astype(jnp.int32), axis=1) == 0
    tail_same = doc_ids == doc_ids[-1]
    causal = positions[:, None] >= positions[None, :]
    allowed = jnp.logical_and(causal, doc_ids[:, None] == doc_ids[None, :])
    return (opened, tail_same, allowed)


def decay_terms(log_decay, opened, tail_same, allowed):
    climb_sum = jnp.cumsum(log_decay, axis=0)
    climb_heads = climb_sum.T
    spread = climb_heads[:, :, None] - climb_heads[:, None, :]
    decay_mask = jnp.where(allowed[None, :, :], jnp.exp(jnp.minimum(spread, 0.0)), 0.0)
    entering_weight = jnp.where(opened[:, None], jnp.exp(climb_sum), 0.0)
    exiting_weight = jnp.where(tail_same[:, None], jnp.exp(climb_sum[-1][None, :] - climb_sum), 0.0)
    carry_decay = entering_weight[-1]
    return (decay_mask, entering_weight, exiting_weight, carry_decay)


def token_sum(left, right):
    return lax.dot_general(
        left, right, (((0,), (0,)), ((), ())), preferred_element_type=jnp.float32
    )


def row_times(left, right):
    return lax.dot_general(
        left, right, (((1,), (1,)), ((), ())), preferred_element_type=jnp.float32
    )


def forward_combine(earlier, latter):
    return (earlier[0] * latter[0], latter[0][:, None, None] * earlier[1] + latter[1])


def backward_combine(earlier, latter):
    return (earlier[0] * latter[0], latter[1] + latter[0][:, None, None] * earlier[1])


def local(
    tokens,
    log_decay,
    starts,
    norm1_gain,
    norm1_bias,
    query_weight,
    key_weight,
    value_weight,
    gate_weight,
    output_weight,
    norm2_gain,
    norm2_bias,
    ffn_gate,
    ffn_up,
    ffn_down,
    cotangent,
):
    row_count = tokens.shape[0]
    feature_count = tokens.shape[1]
    head_count = log_decay.shape[1]
    key_size = query_weight.shape[1] // head_count
    value_size = value_weight.shape[1] // head_count
    share_width = feature_count // lax.axis_size("head")
    share_start = lax.axis_index("head") * share_width
    block_start = lax.axis_index("seq") * row_count
    positions = block_start + jnp.arange(row_count, dtype=jnp.int32)
    opened, tail_same, allowed = links(starts, positions, block_start)
    decay_mask, entering_weight, exiting_weight, carry_decay = decay_terms(
        log_decay, opened, tail_same, allowed
    )
    angles = rotary_angles(positions, key_size)
    inputs_wide = tokens.astype(jnp.float32)
    normed1, norm1_back = jax.vjp(layer_norm, inputs_wide, norm1_gain, norm1_bias)
    normed1_b = normed1.astype(jnp.bfloat16)
    query_rows = jnp.dot(normed1_b, query_weight, preferred_element_type=jnp.float32)
    key_matrix = jnp.dot(normed1_b, key_weight, preferred_element_type=jnp.float32)
    values_b = jnp.dot(normed1_b, value_weight, preferred_element_type=jnp.float32).astype(
        jnp.bfloat16
    )
    gate_act = jnp.dot(normed1_b, gate_weight, preferred_element_type=jnp.float32)
    query_b = rotate(query_rows.reshape(row_count, head_count, key_size), angles).astype(
        jnp.bfloat16
    )
    key_b = (
        rotate(key_matrix.reshape(row_count, head_count, key_size), angles) * key_size ** (-0.5)
    ).astype(jnp.bfloat16)
    value_heads = values_b.reshape(row_count, head_count, value_size)
    scores = jnp.einsum("thk,shk->hts", query_b, key_b, preferred_element_type=jnp.float32)
    weights_b = (scores * decay_mask).astype(jnp.bfloat16)
    key_exiting = key_b.astype(jnp.float32) * exiting_weight[:, :, None]
    value_expanded = value_heads.astype(jnp.float32)
    segment_state = jnp.einsum(
        "zbe,zbc->bec", key_exiting, value_expanded, precision=maximal_precision
    )
    incoming_state = prefix(
        (carry_decay, segment_state),
        "seq",
        forward_combine,
        (jnp.ones_like(carry_decay), jnp.zeros_like(segment_state)),
        False,
    )[1]
    query_entering = query_b.astype(jnp.float32) * entering_weight[:, :, None]
    retention_output = jnp.einsum(
        "hts,shv->thv", weights_b, value_heads, preferred_element_type=jnp.float32
    )
    retention_output = retention_output + jnp.einsum(
        "wrj,rjd->wrd", query_entering, incoming_state, precision=maximal_precision
    )

    def gate_mix(retained_in, gate_in):
        return jax.nn.silu(gate_in) * group_norm(retained_in).reshape(
            row_count, head_count * value_size
        )

    mixed, mix_back = jax.vjp(gate_mix, retention_output, gate_act)
    mixed_b = mixed.astype(jnp.bfloat16)
    branch = lax.psum(
        jnp.dot(mixed_b, output_weight, preferred_element_type=jnp.float32).astype(jnp.bfloat16),
        "head",
    ).astype(jnp.float32)
    resid = inputs_wide + branch
    normed2, norm2_back = jax.vjp(layer_norm, resid, norm2_gain, norm2_bias)
    normed2_b = normed2.astype(jnp.bfloat16)
    gate_ff = jnp.dot(normed2_b, ffn_gate, preferred_element_type=jnp.float32)
    up_ff = jnp.dot(normed2_b, ffn_up, preferred_element_type=jnp.float32)

    def gated_unit(gate_in, up_in):
        return jax.nn.gelu(gate_in, approximate=False) * up_in

    hidden, unit_back = jax.vjp(gated_unit, gate_ff, up_ff)
    hidden_b = hidden.astype(jnp.bfloat16)
    ffn_out = lax.psum_scatter(
        jnp.dot(hidden_b, ffn_down, preferred_element_type=jnp.float32).astype(jnp.bfloat16),
        "head",
        scatter_dimension=1,
        tiled=True,
    ).astype(jnp.float32)
    resid_share = lax.dynamic_slice_in_dim(resid, share_start, share_width, 1)
    output = (resid_share + ffn_out).astype(jnp.bfloat16)
    grad_rows = lax.all_gather(cotangent, "head", axis=1, tiled=True)
    down_grad = token_sum(grad_rows, hidden_b)
    hidden_grad = row_times(grad_rows, ffn_down)
    gate_ff_grad, up_ff_grad = unit_back(hidden_grad)
    gate_ff_b = gate_ff_grad.astype(jnp.bfloat16)
    up_ff_b = up_ff_grad.astype(jnp.bfloat16)
    ffn_gate_grad = token_sum(normed2_b, gate_ff_b)
    ffn_up_grad = token_sum(normed2_b, up_ff_b)
    normed2_grad = lax.psum(
        (row_times(gate_ff_b, ffn_gate) + row_times(up_ff_b, ffn_up)).astype(jnp.bfloat16), "head"
    ).astype(jnp.float32)
    resid_norm_grad, norm2_gain_grad, norm2_bias_grad = norm2_back(normed2_grad)
    resid_grad = grad_rows.astype(jnp.float32) + resid_norm_grad
    branch_grad_b = resid_grad.astype(jnp.bfloat16)
    output_grad = token_sum(branch_grad_b, mixed_b)
    mixed_grad = row_times(branch_grad_b, output_weight)
    retained_grad, gate_grad = mix_back(mixed_grad)
    gate_grad_b = gate_grad.astype(jnp.bfloat16)
    retained_grad_b = retained_grad.astype(jnp.bfloat16)
    retention_gradient_expanded = retained_grad_b.astype(jnp.float32)
    weight_grad = jnp.einsum(
        "thv,shv->hts", retained_grad_b, value_heads, preferred_element_type=jnp.float32
    )
    score_grad_b = (weight_grad * decay_mask).astype(jnp.bfloat16)
    segment_state_gradient = jnp.einsum(
        "noj,nos->ojs", query_entering, retention_gradient_expanded, precision=maximal_precision
    )
    outgoing_state_gradient = prefix(
        (carry_decay, segment_state_gradient),
        "seq",
        backward_combine,
        (jnp.ones_like(carry_decay), jnp.zeros_like(segment_state_gradient)),
        True,
    )[1]
    query_rot_grad = jnp.einsum(
        "hts,shk->thk", score_grad_b, key_b, preferred_element_type=jnp.float32
    )
    query_rot_grad = query_rot_grad + entering_weight[:, :, None] * jnp.einsum(
        "iob,oxb->iox", retention_gradient_expanded, incoming_state, precision=maximal_precision
    )
    key_rot_grad = jnp.einsum(
        "hts,thk->shk", score_grad_b, query_b, preferred_element_type=jnp.float32
    )
    key_rot_grad = key_rot_grad + exiting_weight[:, :, None] * jnp.einsum(
        "men,egn->meg", value_expanded, outgoing_state_gradient, precision=maximal_precision
    )
    values_grad = jnp.einsum(
        "hts,thv->shv", weights_b, retained_grad_b, preferred_element_type=jnp.float32
    )
    values_grad = values_grad + jnp.einsum(
        "mug,ugi->mui", key_exiting, outgoing_state_gradient, precision=maximal_precision
    )
    query_grad_b = (
        rotate_back(query_rot_grad, angles)
        .reshape(row_count, head_count * key_size)
        .astype(jnp.bfloat16)
    )
    key_grad_b = (
        (rotate_back(key_rot_grad, angles) * key_size ** (-0.5))
        .reshape(row_count, head_count * key_size)
        .astype(jnp.bfloat16)
    )
    value_grad_b = values_grad.reshape(row_count, head_count * value_size).astype(jnp.bfloat16)
    query_weight_grad = token_sum(normed1_b, query_grad_b)
    key_weight_grad = token_sum(normed1_b, key_grad_b)
    value_weight_grad = token_sum(normed1_b, value_grad_b)
    gate_weight_grad = token_sum(normed1_b, gate_grad_b)
    normed1_partial = row_times(query_grad_b, query_weight) + row_times(key_grad_b, key_weight)
    normed1_partial = (
        normed1_partial
        + row_times(value_grad_b, value_weight)
        + row_times(gate_grad_b, gate_weight)
    )
    normed1_grad = lax.psum(normed1_partial.astype(jnp.bfloat16), "head").astype(jnp.float32)
    input_norm_grad, norm1_gain_grad, norm1_bias_grad = norm1_back(normed1_grad)
    input_full = resid_grad + input_norm_grad
    input_grad = lax.dynamic_slice_in_dim(input_full, share_start, share_width, 1).astype(
        jnp.bfloat16
    )
    every_sum = (
        lax.psum_scatter(query_weight_grad, "seq", scatter_dimension=0, tiled=True),
        lax.psum_scatter(key_weight_grad, "seq", scatter_dimension=0, tiled=True),
        lax.psum_scatter(value_weight_grad, "seq", scatter_dimension=0, tiled=True),
        lax.psum_scatter(gate_weight_grad, "seq", scatter_dimension=0, tiled=True),
        lax.psum_scatter(output_grad, "seq", scatter_dimension=0, tiled=True),
        lax.psum_scatter(norm1_gain_grad, "seq", scatter_dimension=0, tiled=True),
        lax.psum_scatter(norm1_bias_grad, "seq", scatter_dimension=0, tiled=True),
        lax.psum_scatter(ffn_gate_grad, "seq", scatter_dimension=0, tiled=True),
        lax.psum_scatter(ffn_up_grad, "seq", scatter_dimension=0, tiled=True),
        lax.psum_scatter(down_grad, "seq", scatter_dimension=0, tiled=True),
        lax.psum_scatter(norm2_gain_grad, "seq", scatter_dimension=0, tiled=True),
        lax.psum_scatter(norm2_bias_grad, "seq", scatter_dimension=0, tiled=True),
    )
    branch_summed = every_sum[:7]
    ffn_summed = every_sum[7:]
    return (
        output,
        input_grad,
        branch_summed[5],
        branch_summed[6],
        branch_summed[0],
        branch_summed[1],
        branch_summed[2],
        branch_summed[3],
        branch_summed[4].T,
        ffn_summed[3],
        ffn_summed[4],
        ffn_summed[0],
        ffn_summed[1],
        ffn_summed[2].T,
    )


def solution(mesh):
    return jax.shard_map(
        local,
        mesh=mesh,
        in_specs=(
            P("seq", None),
            P("seq", "head"),
            P(),
            P(),
            P(),
            P(None, "head"),
            P(None, "head"),
            P(None, "head"),
            P(None, "head"),
            P("head", None),
            P(),
            P(),
            P(None, "head"),
            P(None, "head"),
            P("head", None),
            P("seq", "head"),
        ),
        out_specs=(
            P("seq", "head"),
            P("seq", "head"),
            P("seq"),
            P("seq"),
            P("seq", "head"),
            P("seq", "head"),
            P("seq", "head"),
            P("seq", "head"),
            P("head", "seq"),
            P("seq"),
            P("seq"),
            P("seq", "head"),
            P("seq", "head"),
            P("head", "seq"),
        ),
        check_vma=False,
    )
```

profile of v0, /device:TPU:0, one launch (start us, length us, event | category | flops | bytes accessed | tf_op | source)
XLA Modules:
  0.0 3454.6 jit_solution(7270808613570527768)
XLA Ops:
  44.4 82.6 %all-gather.2 = bf16[64,1,2]{2,1,0:T(2,128)(2,1)S(1)} all-gather(bf16[1,1,2]{2,1,0:T(2,128)(2,1)S(1)} %bitcast.170), channel_id=1, replica_groups=mesh['seq'=64,'head'=2] {'seq'}, dimensions={0}, use_global_device_ids=true | all-gather | bytes 260 | tf_op jit(solution)/shard_map/all_gather | solution.py:15
  137.2 69.7 %all-gather.9.cloned.1.call-done = bf16[128,256,432]{1,2,0:T(8,128)(2,1)} async-done(((bf16[2,256,432]{1,2,0:T(8,128)(2,1)}), bf16[128,256,432]{1,2,0:T(8,128)(2,1)}) %all-gather.9.cloned.1.call-update) | async-done | bytes 28311568 | tf_op jit(solution)/shard_map/all_gather | solution.py:15
  206.9 224.6 %while.30 = (s32[]{:T(128)}, f32[2,256,432]{2,1,0:T(8,128)S(1)}, s32[]{:T(128)}, bf16[64,2]{1,0:T(8,128)(2,1)S(1)}, bf16[64,2,256,432]{2,3,1,0:T(8,128)(2,1)}, /*index=5*/s32[]{:T(128)}, s32[]{:T(128)}) while((s32[]{:T(128)}, f32[2,256,432]{2,1,0:T(8,128)S(1)}, s32[]{:T(128)}, bf16[64,2]{1,0:T(8,128)(2,1)S(1)}, ...), condition=%wide.region_7.8_spmd.clone, body=%wide.region_6.7_spmd.clone.sunk | while | flops 1105926 | bytes 3981445 | solution.py:33
  431.5 9.4 bitcast_reduce_fusion
  453.2 10.4 all-reduce.11.cloned.1.call-start
  463.6 55.1 %all-reduce.9.cloned.1.call-done = bf16[896,1024]{1,0:T(8,128)(2,1)} async-done(((bf16[896,1024]{1,0:T(8,128)(2,1)}), bf16[896,1024]{1,0:T(8,128)(2,1)}) %all-reduce.9.cloned.1.call-update) | async-done | bytes 1835024 | tf_op jit(solution)/shard_map/psum | solution.py:205
  528.6 25.5 all-gather.7.cloned.1.call-done
  554.1 10.3 multiply_convert_fusion.2
  574.9 64.2 %all-reduce.11.cloned.1.call-done = bf16[896,1024]{1,0:T(8,128)(2,1)} async-done(((bf16[896,1024]{1,0:T(8,128)(2,1)}), bf16[896,1024]{1,0:T(8,128)(2,1)}) %all-reduce.11.cloned.1.call-update) | async-done | bytes 1835024 | tf_op jit(solution)/shard_map/psum | solution.py:236
  683.7 136.5 %all-gather.11.cloned.1.call-done = bf16[128,256,432]{1,2,0:T(8,128)(2,1)} async-done(((bf16[2,256,432]{1,2,0:T(8,128)(2,1)}), bf16[128,256,432]{1,2,0:T(8,128)(2,1)}) %all-gather.11.cloned.1.call-update) | async-done | bytes 28311568 | tf_op jit(solution)/shard_map/all_gather | solution.py:15
  820.2 224.3 %while.31 = (s32[]{:T(128)}, f32[2,256,432]{2,1,0:T(8,128)S(1)}, s32[]{:T(128)}, bf16[64,2,256,432]{2,3,1,0:T(8,128)(2,1)}, bf16[64,2]{1,0:T(8,128)(2,1)S(1)}, /*index=5*/s32[]{:T(128)}, s32[]{:T(128)}, s32[]{:T(128)}, s32[]{:T(128)}) while((s32[]{:T(128)}, f32[2,256,432]{2,1,0:T(8,128)S(1)}, s32[]{:T(128)}, ...), condition=%wide.region_20.21_spmd.clone, body=%wide.region_19.20_spmd.clone.sunk | while | flops 1105930 | bytes 3981507 | solution.py:33
  1061.9 7.1 add_convert_fusion.3
  1092.0 6.2 fusion.76
  1098.3 6.8 fusion.38
  1120.4 6.2 fusion.73
  1131.5 9.7 all-reduce.13.cloned.1.call-done
  1144.7 279.4 %all-reduce.4 = (f32[1024]{0:T(1024)S(1)}, f32[1024]{0:T(1024)S(1)}, f32[1024]{0:T(1024)S(1)}, f32[1024]{0:T(1024)S(1)}) all-reduce(f32[1024]{0:T(1024)S(1)} %get-tuple-element.400, f32[1024]{0:T(1024)S(1)} %get-tuple-element.404, f32[1024]{0:T(1024)S(1)} %get-tuple-element.398, ...), channel_id=5, replica_groups=mesh['seq'=64,'head'=2] {'seq'}, use_global_device_ids=true, to_apply=%region_25.26.clone | all-reduce | flops 4096 | bytes 32768
  1433.6 288.6 %reduce-scatter.24.cloned.1.call-done = f32[16,864]{1,0:T(8,128)} async-done(((f32[1024,864]{1,0:T(8,128)}), f32[16,864]{1,0:T(8,128)}) %reduce-scatter.24.cloned.1.call-update) | async-done | bytes 55312 | tf_op jit(solution)/shard_map/reduce_scatter | solution.py:315
  1722.2 288.2 %reduce-scatter.26.cloned.1.call-done = f32[16,864]{1,0:T(8,128)} async-done(((f32[1024,864]{1,0:T(8,128)}), f32[16,864]{1,0:T(8,128)}) %reduce-scatter.26.cloned.1.call-update) | async-done | bytes 55312 | tf_op jit(solution)/shard_map/reduce_scatter | solution.py:316
  2010.4 288.5 %reduce-scatter.22.cloned.1.call-done = f32[16,864]{1,0:T(8,128)} async-done(((f32[1024,864]{1,0:T(8,128)}), f32[16,864]{1,0:T(8,128)}) %reduce-scatter.22.cloned.1.call-update) | async-done | bytes 55312 | tf_op jit(solution)/shard_map/reduce_scatter | solution.py:312
  2299.0 288.2 %reduce-scatter.20.cloned.1.call-done = f32[16,864]{1,0:T(8,128)} async-done(((f32[1024,864]{1,0:T(8,128)}), f32[16,864]{1,0:T(8,128)}) %reduce-scatter.20.cloned.1.call-update) | async-done | bytes 55312 | tf_op jit(solution)/shard_map/reduce_scatter | solution.py:311
  2587.2 285.0 %reduce-scatter.14.cloned.1.call-done = f32[16,512]{1,0:T(8,128)} async-done(((f32[1024,512]{1,0:T(8,128)}), f32[16,512]{1,0:T(8,128)}) %reduce-scatter.14.cloned.1.call-update) | async-done | bytes 32784 | tf_op jit(solution)/shard_map/reduce_scatter | solution.py:308
  2872.2 286.4 %reduce-scatter.16.cloned.1.call-done = f32[16,512]{1,0:T(8,128)} async-done(((f32[1024,512]{1,0:T(8,128)}), f32[16,512]{1,0:T(8,128)}) %reduce-scatter.16.cloned.1.call-update) | async-done | bytes 32784 | tf_op jit(solution)/shard_map/reduce_scatter | solution.py:309
  3158.6 289.2 %reduce-scatter.18.cloned.1.call-done = f32[16,864]{1,0:T(8,128)} async-done(((f32[1024,864]{1,0:T(8,128)}), f32[16,864]{1,0:T(8,128)}) %reduce-scatter.18.cloned.1.call-update) | async-done | bytes 55312 | tf_op jit(solution)/shard_map/reduce_scatter | solution.py:310
  (798 shorter events, 639.7 us)
Async XLA Ops:
  7.2 546.9 %copy-start = (bf16[864,1024]{1,0:T(8,128)(2,1)S(1)}, bf16[864,1024]{1,0:T(8,128)(2,1)}, u32[]{:S(2)}) copy-start(bf16[864,1024]{1,0:T(8,128)(2,1)} %param.34) | copy-start | bytes 5308420
  7.2 199.7 %all-gather.9.cloned.1.call-start = ((), (), s32[]{:S(2)}) async-start(), calls=%async_computation.21 | async-start | bytes 28753920 | tf_op jit(solution)/shard_map/all_gather | solution.py:15
  40.4 87.8 %copy-start.24 = (bf16[896,2,128]{2,0,1:T(8,128)(2,1)}, bf16[896,2,128]{2,0,1:T(8,128)(2,1)S(1)}, u32[]{:S(2)}) copy-start(bf16[896,2,128]{2,0,1:T(8,128)(2,1)S(1)} %get-tuple-element.447) | copy-start | bytes 1376260
  44.1 474.6 %all-reduce.9.cloned.1.call-start = ((), (), s32[]{:S(2)}) async-start(), calls=%async_computation.9 | async-start | bytes 3670016 | tf_op jit(solution)/shard_map/psum | solution.py:205
  452.4 101.6 %all-gather.7.cloned.1.call-start = ((), (), s32[]{:S(2)}) async-start(), calls=%async_computation.11 | async-start | bytes 2752512 | tf_op jit(solution)/shard_map/all_gather | solution.py:228
  453.2 69.6 %copy-start.51 = (f32[1024]{0:T(1024)S(1)}, f32[1024]{0:T(1024)}, u32[]{:S(2)}) copy-start(f32[1024]{0:T(1024)} %param.30) | copy-start | bytes 12292
  453.2 69.5 %copy-start.58 = (f32[1024]{0:T(1024)S(1)}, f32[1024]{0:T(1024)}, u32[]{:S(2)}) copy-start(f32[1024]{0:T(1024)} %param.31) | copy-start | bytes 12292
  453.2 185.9 %all-reduce.11.cloned.1.call-start = ((), (), s32[]{:S(2)}) async-start(), calls=%async_computation.12 | async-start | bytes 3670016 | tf_op jit(solution)/shard_map/psum | solution.py:236
  574.4 245.8 %all-gather.11.cloned.1.call-start = ((), (), s32[]{:S(2)}) async-start(), calls=%async_computation.22 | async-start | bytes 28753920 | tf_op jit(solution)/shard_map/all_gather | solution.py:15
  660.8 467.6 %reduce-scatter.12.cloned.1.call-start = ((), (), s32[]{:S(2)}) async-start(), calls=%async_computation.10 | async-start | bytes 2752512 | tf_op jit(solution)/shard_map/reduce_scatter | solution.py:220
  665.8 475.4 %all-reduce.13.cloned.1.call-start = ((), (), s32[]{:S(2)}) async-start(), calls=%async_computation.13 | async-start | bytes 3670016 | tf_op jit(solution)/shard_map/psum | solution.py:301
  681.3 138.9 %copy-start.8 = (f32[2,256,432]{2,1,0:T(8,128)S(1)}, f32[2,256,432]{2,1,0:T(8,128)}, u32[]{:S(2)}) copy-start(f32[2,256,432]{2,1,0:T(8,128)} %custom-call.1) | copy-start | bytes 2654212
  1074.8 358.8 %reduce-scatter.28.cloned.1.call-start = ((), (), s32[]{:S(2)}) async-start(), calls=%async_computation.23 | async-start | bytes 3727360
  1085.8 636.4 %reduce-scatter.24.cloned.1.call-start = ((), (), s32[]{:S(2)}) async-start(), calls=%async_computation.19 | async-start | bytes 3727360 | tf_op jit(solution)/shard_map/reduce_scatter | solution.py:315
  1092.0 918.5 %reduce-scatter.26.cloned.1.call-start = ((), (), s32[]{:S(2)}) async-start(), calls=%async_computation.20 | async-start | bytes 3727360 | tf_op jit(solution)/shard_map/reduce_scatter | solution.py:316
  1098.2 1200.7 %reduce-scatter.22.cloned.1.call-start = ((), (), s32[]{:S(2)}) async-start(), calls=%async_computation.18 | async-start | bytes 3727360 | tf_op jit(solution)/shard_map/reduce_scatter | solution.py:312
  1105.1 1482.1 %reduce-scatter.20.cloned.1.call-start = ((), (), s32[]{:S(2)}) async-start(), calls=%async_computation.17 | async-start | bytes 3727360 | tf_op jit(solution)/shard_map/reduce_scatter | solution.py:311
  1111.3 1760.9 %reduce-scatter.14.cloned.1.call-start = ((), (), s32[]{:S(2)}) async-start(), calls=%async_computation.14 | async-start | bytes 2129920 | tf_op jit(solution)/shard_map/reduce_scatter | solution.py:308
  1115.7 2042.9 %reduce-scatter.16.cloned.1.call-start = ((), (), s32[]{:S(2)}) async-start(), calls=%async_computation.15 | async-start | bytes 2129920 | tf_op jit(solution)/shard_map/reduce_scatter | solution.py:309
  1120.3 2327.5 %reduce-scatter.18.cloned.1.call-start = ((), (), s32[]{:S(2)}) async-start(), calls=%async_computation.16 | async-start | bytes 3727360 | tf_op jit(solution)/shard_map/reduce_scatter | solution.py:310
  1126.5 14.7 copy-start.48
  1126.5 14.7 copy-start.50
  1126.6 14.7 copy-start.53
  1128.5 298.0 %copy-start.55 = (f32[896]{0:T(1024)S(1)}, f32[896]{0:T(1024)}, u32[]{:S(2)}) copy-start(f32[896]{0:T(1024)} %copy-done.54) | copy-start | bytes 10756
  (68 other events, 255.8 us)
Sparse Core Ops, SparseCore 0:
  44.2 162.6 all-gather.8
  452.5 66.1 all-reduce.8
  520.5 33.5 all-gather.6
  574.5 64.5 all-reduce.10
  661.0 159.1 all-gather.10
  822.4 33.9 reduce-scatter.11
  1074.9 66.2 all-reduce.12
  1144.2 289.4 reduce-scatter.27
  1436.7 285.4 reduce-scatter.23
  1725.0 285.3 reduce-scatter.25
  2013.5 285.4 reduce-scatter.21
  2301.8 285.3 reduce-scatter.19
  2590.2 281.8 reduce-scatter.13
  2875.0 283.5 reduce-scatter.15
  3161.5 286.2 reduce-scatter.17
where the time goes:
time: 3470 us; the launch traced here: 3450 us
  waiting for transfers between devices  2380 us (69%)
  local copies, waits for them, and re-layouts  428 us (12%)
  blocking collectives  362 us (10%)
  matrix products  153 us (4%)
  other arithmetic  100 us (3%)
    dynamic_slice x256, local copies, waits for them, and re-layouts, step(): part[at].astype(own.dtype)  388 us
    reduce_scatter x1, waiting for transfers between devices, local(): lax.psum_scatter(value_weight_grad, 'seq', scatter_dimension=0, tiled=True)  289 us
    reduce_scatter x1, waiting for transfers between devices, local(): lax.psum_scatter(ffn_gate_grad, 'seq', scatter_dimension=0, tiled=True)  289 us
    reduce_scatter x1, waiting for transfers between devices, local(): lax.psum_scatter(output_grad, 'seq', scatter_dimension=0, tiled=True)  289 us
    reduce_scatter x1, waiting for transfers between devices, local(): lax.psum_scatter(gate_weight_grad, 'seq', scatter_dimension=0, tiled=True)  288 us
    reduce_scatter x1, waiting for transfers between devices, local(): lax.psum_scatter(ffn_up_grad, 'seq', scatter_dimension=0, tiled=True)  288 us
    reduce_scatter x1, waiting for transfers between devices, local(): lax.psum_scatter(key_weight_grad, 'seq', scatter_dimension=0, tiled=True)  286 us
    reduce_scatter x1, waiting for transfers between devices, local(): lax.psum_scatter(query_weight_grad, 'seq', scatter_dimension=0, tiled=True)  285 us
  transfers between devices with their start and end apart: 15, of which 14 were waited for; matrix products, arithmetic and copies ran while one was open for 10% of the time, Pallas kernels for 0%

commit v1 on v0

v1 whole, which is shorter than its diff:
```python
import math

import jax
import jax.numpy as jnp
from jax import lax
from jax.sharding import Mesh, PartitionSpec as P

eps_norm = 1e-05
bf16 = jnp.bfloat16
f32 = jnp.float32
SEQ = ("y", "zlo", "x", "core")
CHIPS = ("y", "zlo", "x")
HEAD = "zhi"
SWAP = [(0, 1), (1, 0)]


def dot(left, right):
    return lax.dot_general(left, right, (((1,), (0,)), ((), ())), preferred_element_type=f32)


def token_sum(left, right):
    return lax.dot_general(left, right, (((0,), (0,)), ((), ())), preferred_element_type=f32)


def row_times(left, right):
    return lax.dot_general(left, right, (((1,), (1,)), ((), ())), preferred_element_type=f32)


def norm_stats(values):
    average = jnp.mean(values, axis=-1, keepdims=True)
    centred = values - average
    variance = jnp.mean(centred * centred, axis=-1, keepdims=True)
    inverse = lax.rsqrt(variance + eps_norm)
    return centred * inverse, inverse


def norm_back(xhat, inverse, grad):
    first = jnp.mean(grad, axis=-1, keepdims=True)
    second = jnp.mean(grad * xhat, axis=-1, keepdims=True)
    return inverse * (grad - first - xhat * second)


def swap_heads(array):
    return lax.ppermute(array, HEAD, SWAP)


def rotate(vectors, cosine, sine):
    upper, lower = vectors[:, : cosine.shape[1]], vectors[:, cosine.shape[1] :]
    return jnp.concatenate([upper * cosine - lower * sine, lower * cosine + upper * sine], axis=1)


def split3(values):
    first = values.astype(bf16)
    rest = values - first.astype(f32)
    second = rest.astype(bf16)
    third = (rest - second.astype(f32)).astype(bf16)
    return first, second, third


def block_weights(log_totals, starts, row_count, head):
    blocks = log_totals.shape[0]
    begin = jnp.arange(blocks, dtype=jnp.int32) * row_count
    has_start = jnp.any(
        (starts[None, :] >= begin[:, None]) & (starts[None, :] < begin[:, None] + row_count), axis=1
    )
    own = jnp.where(head == 0, log_totals[:, 0], log_totals[:, 1])
    index = jnp.arange(blocks, dtype=jnp.int32)
    inner = (index[None, :, None] < index[None, None, :]) & (
        index[None, None, :] < index[:, None, None]
    )
    logs = jnp.sum(jnp.where(inner, own[None, None, :], 0.0), axis=2)
    broken = jnp.any(inner & has_start[None, None, :], axis=2)
    later = index[:, None] > index[None, :]
    return jnp.where(later & ~broken, jnp.exp(logs), 0.0)


def local(
    tokens,
    log_decay,
    starts,
    norm1_gain,
    norm1_bias,
    query_weight,
    key_weight,
    value_weight,
    gate_weight,
    output_weight,
    norm2_gain,
    norm2_bias,
    ffn_gate,
    ffn_up,
    ffn_down,
    cotangent,
):
    rows, width = tokens.shape
    heads = log_decay.shape[1]
    dk = query_weight.shape[1] // heads
    dv = value_weight.shape[1] // heads
    half = width // 2
    blocks = lax.axis_size(SEQ)
    seq_at = lax.axis_index(SEQ)
    head_at = lax.axis_index(HEAD)
    core_at = lax.axis_index("core")
    first_head = head_at == 0
    block_start = seq_at * rows
    key_scale = dk ** (-0.5)

    other_cot = swap_heads(cotangent)

    positions = block_start + jnp.arange(rows, dtype=jnp.int32)
    started = starts[None, :] <= positions[:, None]
    doc_ids = jnp.sum(started.astype(jnp.int32), axis=1)
    inside = jnp.logical_and(starts[None, :] >= block_start, started)
    opened = jnp.sum(inside.astype(jnp.int32), axis=1) == 0
    tail_same = doc_ids == doc_ids[-1]
    allowed = (positions[:, None] >= positions[None, :]) & (doc_ids[:, None] == doc_ids[None, :])
    climb = jnp.cumsum(log_decay, axis=0)
    climb_rows = climb.T
    total = climb[-1]
    entering = jnp.where(opened[:, None], jnp.exp(climb), 0.0)
    leaving = jnp.where(tail_same[:, None], jnp.exp(total[None, :] - climb), 0.0)
    masks = [
        jnp.where(
            allowed,
            jnp.exp(jnp.minimum(climb[:, h : h + 1] - climb_rows[h : h + 1, :], 0.0)),
            0.0,
        )
        for h in range(heads)
    ]
    frequency = jnp.exp(-math.log(10000.0) * jnp.arange(dk // 2, dtype=f32) / (dk // 2))
    angles = positions.astype(f32)[:, None] * frequency[None, :]
    cosine, sine = jnp.cos(angles), jnp.sin(angles)

    wide = tokens.astype(f32)
    xhat1, inverse1 = norm_stats(wide)
    normed1 = (xhat1 * norm1_gain + norm1_bias).astype(bf16)
    keys, values, queries, gates, exits = [], [], [], [], []
    value_parts = [value_weight[:, h * dv : (h + 1) * dv] for h in range(heads)]
    gate_parts = [gate_weight[:, h * dv : (h + 1) * dv] for h in range(heads)]
    for h in range(heads):
        rows_k = dot(normed1, key_weight[:, h * dk : (h + 1) * dk])
        key = (rotate(rows_k, cosine, sine) * key_scale).astype(bf16)
        keys.append(key)
        values.append(dot(normed1, value_parts[h]).astype(bf16))
        exits.append((key.astype(f32) * leaving[:, h : h + 1]).astype(bf16))
    states = jnp.concatenate([token_sum(exits[h], values[h]) for h in range(heads)], axis=0)
    pieces = states.astype(bf16).reshape(blocks, heads * dk // blocks, dv)
    marks = jnp.concatenate([part for part in split3(total)])
    marks = jnp.broadcast_to(
        jnp.pad(marks, (0, 128 - 3 * heads - dv % 128))[None, None, :],
        (blocks, pieces.shape[1], 128 - dv % 128),
    )
    arrived = lax.all_to_all(jnp.concatenate([pieces, marks], axis=2), SEQ, 0, 0, tiled=True)
    tags = arrived[:, 0, dv : dv + 3 * heads].astype(f32)
    log_totals = tags[:, :heads] + tags[:, heads : 2 * heads] + tags[:, 2 * heads :]
    piece_head = seq_at // (blocks // heads)
    carried = block_weights(log_totals, starts, rows, piece_head).astype(bf16)
    summed = lax.dot_general(
        carried, arrived[:, :, :dv], (((1,), (0,)), ((), ())), preferred_element_type=f32
    ).astype(bf16)
    incoming = lax.all_to_all(summed, SEQ, 0, 0, tiled=True).reshape(heads * dk, dv)

    mixed, ghats, ginvs, weights = [], [], [], []
    branch = None
    output_parts = [output_weight[h * dv : (h + 1) * dv] for h in range(heads)]
    for h in range(heads):
        rows_q = dot(normed1, query_weight[:, h * dk : (h + 1) * dk])
        query = rotate(rows_q, cosine, sine).astype(bf16)
        queries.append(query)
        gates.append(dot(normed1, gate_parts[h]))
        weight = (row_times(query, keys[h]) * masks[h]).astype(bf16)
        weights.append(weight)
        retained = dot(weight, values[h])
        retained = retained + entering[:, h : h + 1] * dot(query, incoming[h * dk : (h + 1) * dk])
        ghat, ginv = norm_stats(retained)
        ghats.append(ghat)
        ginvs.append(ginv)
        mix = (jax.nn.silu(gates[h]) * ghat).astype(bf16)
        mixed.append(mix)
        part = dot(mix, output_parts[h])
        branch = part if branch is None else branch + part
    branch = branch.astype(bf16)
    resid = wide + branch.astype(f32) + swap_heads(branch).astype(f32)

    xhat2, inverse2 = norm_stats(resid)
    normed2 = (xhat2 * norm2_gain + norm2_bias).astype(bf16)
    gate_ff = dot(normed2, ffn_gate)
    up_ff = dot(normed2, ffn_up)
    cdf = 0.5 * (1.0 + lax.erf(gate_ff * (0.5**0.5)))
    gelu = gate_ff * cdf
    hidden = (gelu * up_ff).astype(bf16)
    ffn_out = dot(hidden, ffn_down).astype(bf16)
    low, high = ffn_out[:, :half], ffn_out[:, half:]
    arrived_out = swap_heads(jnp.where(first_head, high, low))
    own_resid = jnp.where(first_head, resid[:, :half], resid[:, half:])
    output = (
        own_resid + (jnp.where(first_head, low, high).astype(f32) + arrived_out.astype(f32))
    ).astype(bf16)

    cot = jnp.concatenate(
        [
            jnp.where(first_head, cotangent, other_cot),
            jnp.where(first_head, other_cot, cotangent),
        ],
        axis=1,
    )
    hidden_grad = row_times(cot, ffn_down)
    pdf = (1.0 / math.sqrt(2.0 * math.pi)) * jnp.exp(-0.5 * gate_ff * gate_ff)
    gate_ff_grad = (hidden_grad * up_ff * (cdf + gate_ff * pdf)).astype(bf16)
    up_ff_grad = (hidden_grad * gelu).astype(bf16)
    normed2_part = (row_times(gate_ff_grad, ffn_gate) + row_times(up_ff_grad, ffn_up)).astype(bf16)
    normed2_grad = normed2_part.astype(f32) + swap_heads(normed2_part).astype(f32)
    gain2_grad = jnp.sum(normed2_grad * xhat2, axis=0)
    bias2_grad = jnp.sum(normed2_grad, axis=0)
    resid_grad = cot.astype(f32) + norm_back(xhat2, inverse2, normed2_grad * norm2_gain)
    branch_grad = resid_grad.astype(bf16)

    gate_grads, retained_grads, state_parts = [], [], []
    for h in range(heads):
        mixed_grad = row_times(branch_grad, output_parts[h])
        sig = jax.nn.sigmoid(gates[h])
        gate_grads.append(
            (mixed_grad * ghats[h] * (sig * (1.0 + gates[h] * (1.0 - sig)))).astype(bf16)
        )
        retained_grad = norm_back(ghats[h], ginvs[h], mixed_grad * (gates[h] * sig)).astype(bf16)
        retained_grads.append(retained_grad)
        scaled = (queries[h].astype(f32) * entering[:, h : h + 1]).astype(bf16)
        state_parts.append(token_sum(scaled, retained_grad))
    pieces = jnp.concatenate(state_parts, axis=0).astype(bf16)
    pieces = pieces.reshape(blocks, heads * dk // blocks, dv)
    arrived_back = lax.all_to_all(pieces, SEQ, 0, 0, tiled=True)
    summed_back = lax.dot_general(
        carried, arrived_back, (((0,), (0,)), ((), ())), preferred_element_type=f32
    ).astype(bf16)
    outgoing = lax.all_to_all(summed_back, SEQ, 0, 0, tiled=True).reshape(heads * dk, dv)

    query_grads, key_grads, value_grads = [], [], []
    for h in range(heads):
        rg = retained_grads[h]
        out_state = outgoing[h * dk : (h + 1) * dk]
        in_state = incoming[h * dk : (h + 1) * dk]
        score_grad = (row_times(rg, values[h]) * masks[h]).astype(bf16)
        query_rot = dot(score_grad, keys[h]) + entering[:, h : h + 1] * row_times(rg, in_state)
        key_rot = token_sum(score_grad, queries[h]) + leaving[:, h : h + 1] * row_times(
            values[h], out_state
        )
        value_grad = token_sum(weights[h], rg) + leaving[:, h : h + 1] * dot(keys[h], out_state)
        query_grads.append(rotate(query_rot, cosine, -sine).astype(bf16))
        key_grads.append((rotate(key_rot, cosine, -sine) * key_scale).astype(bf16))
        value_grads.append(value_grad.astype(bf16))
    normed1_part = None
    for h in range(heads):
        for grad, weight in (
            (query_grads[h], query_weight[:, h * dk : (h + 1) * dk]),
            (key_grads[h], key_weight[:, h * dk : (h + 1) * dk]),
            (value_grads[h], value_parts[h]),
            (gate_grads[h], gate_parts[h]),
        ):
            part = row_times(grad, weight)
            normed1_part = part if normed1_part is None else normed1_part + part
    normed1_part = normed1_part.astype(bf16)
    low, high = normed1_part[:, :half], normed1_part[:, half:]
    arrived_grad = swap_heads(jnp.where(first_head, high, low))
    normed1_grad = jnp.where(first_head, low, high).astype(f32) + arrived_grad.astype(f32)
    own_hat = jnp.where(first_head, xhat1[:, :half], xhat1[:, half:])
    own_gain = jnp.where(first_head, norm1_gain[:half], norm1_gain[half:])
    scaled_grad = normed1_grad * own_gain
    sums = jnp.stack([jnp.sum(scaled_grad, axis=1), jnp.sum(scaled_grad * own_hat, axis=1)])
    sums = (sums + swap_heads(sums)) * (1.0 / width)
    own_back = inverse1 * (scaled_grad - sums[0][:, None] - own_hat * sums[1][:, None])
    own_resid_grad = jnp.where(first_head, resid_grad[:, :half], resid_grad[:, half:])
    input_grad = (own_resid_grad + own_back).astype(bf16)
    own_norm1 = jnp.stack([jnp.sum(normed1_grad * own_hat, axis=0), jnp.sum(normed1_grad, axis=0)])
    other_norm1 = swap_heads(own_norm1)
    norm1_grads = jnp.concatenate(
        [
            jnp.where(first_head, own_norm1, other_norm1),
            jnp.where(first_head, other_norm1, own_norm1),
        ],
        axis=1,
    )
    vectors = jnp.concatenate([norm1_grads, gain2_grad[None], bias2_grad[None]], axis=0)
    vector_high = vectors.astype(bf16)
    vector_low = (vectors - vector_high.astype(f32)).astype(bf16)

    grads = [token_sum(normed1, query_grads[h]).astype(bf16) for h in range(heads)]
    grads += [token_sum(normed1, key_grads[h]).astype(bf16) for h in range(heads)]
    grads += [token_sum(normed1, value_grads[h]).astype(bf16) for h in range(heads)]
    grads += [token_sum(normed1, gate_grads[h]).astype(bf16) for h in range(heads)]
    grads += [token_sum(branch_grad, mixed[h]).astype(bf16) for h in range(heads)]
    grads += [token_sum(normed2, gate_ff_grad).astype(bf16)]
    grads += [token_sum(normed2, up_ff_grad).astype(bf16)]
    grads += [token_sum(cot, hidden).astype(bf16)]
    grads += [vector_high.T, vector_low.T]
    widths = [g.shape[1] for g in grads]
    everything = jnp.concatenate(grads, axis=1)
    everything = everything.reshape(blocks // 2, 2, width // blocks, -1)
    kept = jnp.where(core_at == 0, everything[:, 0], everything[:, 1])
    sent = jnp.where(core_at == 0, everything[:, 1], everything[:, 0])
    got = lax.ppermute(sent, "core", SWAP)
    chip_sum = (kept.astype(f32) + got.astype(f32)).astype(bf16)
    shares = lax.all_to_all(chip_sum, CHIPS, 0, 0, tiled=True)
    whole = jnp.sum(shares.astype(f32), axis=0)
    parts, at = [], 0
    for wide_part in widths:
        parts.append(whole[:, at : at + wide_part])
        at += wide_part
    query_out = jnp.concatenate(parts[0:2], axis=1)
    key_out = jnp.concatenate(parts[2:4], axis=1)
    value_out = jnp.concatenate(parts[4:6], axis=1)
    gate_out = jnp.concatenate(parts[6:8], axis=1)
    output_out = jnp.concatenate(parts[8:10], axis=1).T
    ffn_gate_out, ffn_up_out, ffn_down_out = parts[10], parts[11], parts[12].T
    vector_out = parts[13] + parts[14]
    return (
        output,
        input_grad,
        vector_out[:, 0],
        vector_out[:, 1],
        query_out,
        key_out,
        value_out,
        gate_out,
        output_out,
        vector_out[:, 2],
        vector_out[:, 3],
        ffn_gate_out,
        ffn_up_out,
        ffn_down_out,
    )


def solution(mesh):
    fine = Mesh(mesh.devices.reshape(4, 2, 4, 2, 2), SEQ + (HEAD,))
    return jax.shard_map(
        local,
        mesh=fine,
        in_specs=(
            P(SEQ, None),
            P(SEQ, HEAD),
            P(),
            P(),
            P(),
            P(None, HEAD),
            P(None, HEAD),
            P(None, HEAD),
            P(None, HEAD),
            P(HEAD, None),
            P(),
            P(),
            P(None, HEAD),
            P(None, HEAD),
            P(HEAD, None),
            P(SEQ, HEAD),
        ),
        out_specs=(
            P(SEQ, HEAD),
            P(SEQ, HEAD),
            P(SEQ),
            P(SEQ),
            P(SEQ, HEAD),
            P(SEQ, HEAD),
            P(SEQ, HEAD),
            P(SEQ, HEAD),
            P(HEAD, SEQ),
            P(SEQ),
            P(SEQ),
            P(SEQ, HEAD),
            P(SEQ, HEAD),
            P(HEAD, SEQ),
        ),
        check_vma=False,
    )
```

time: 3470 us -> 593 us (0.17)
  waiting for transfers between devices: 2380 us -> 221 us
  blocking collectives: 362 us -> 0 us
  local copies, waits for them, and re-layouts: 428 us -> 101 us
  starting transfers between devices: 11.9 us -> 62.6 us
  other arithmetic: 100 us -> 61.7 us
    reduce_scatter x8 -> x0, waiting for transfers between devices: 2010 us -> none  [the longest x1 289 us: local(): lax.psum_scatter(value_weight_grad, 'seq', scatter_dimension=0, tiled=True)]
    dynamic_slice x256 -> x0, local copies, waits for them, and re-layouts: 388 us -> none  [step(): part[at].astype(own.dtype)]
    unnamed x1 -> x0, blocking collectives: 279 us -> none
    all_gather x3 -> x0, waiting for transfers between devices: 232 us -> none  [the longest x2 206 us: prefix(): lax.all_gather(part.astype(kind), axis)]
    ppermute x0 -> x8, waiting for transfers between devices: none -> 198 us  [the longest x7 187 us: swap_heads(): return lax.ppermute(array, HEAD, SWAP)]
    psum x3 -> x0, waiting for transfers between devices: 129 us -> none  [the longest x1 64.2 us: local(): lax.psum((row_times(gate_ff_b, ffn_gate) + row_times(up_ff_b, ffn_up)).as...]
    all_gather x1 -> x0, blocking collectives: 82.6 us -> none  [prefix(): lax.all_gather(part.astype(kind), axis)]
    concatenate x1 -> x6, local copies, waits for them, and re-layouts: 2.62 us -> 85.3 us  [the longest x2 82.3 us: local(): everything = jnp.concatenate(grads, axis=1)]
  transfers between devices with their start and end apart: 15 -> 13, of which waited for: 14 -> 9; matrix products, arithmetic and copies ran while one was open for 10% -> 10% of each run, Pallas kernels for 0% -> 0%
where the time goes in v1:
time: 593 us; the launch traced here: 582 us
  waiting for transfers between devices  221 us (37%)
  matrix products  133 us (22%)
  local copies, waits for them, and re-layouts  101 us (17%)
  starting transfers between devices  62.6 us (11%)
  other arithmetic  61.7 us (10%)
    ppermute x7, waiting for transfers between devices, swap_heads(): return lax.ppermute(array, HEAD, SWAP)  187 us
    concatenate x2, local copies, waits for them, and re-layouts, local(): everything = jnp.concatenate(grads, axis=1)  82.3 us
    dot_general x21, matrix products, row_times(): lax.dot_general(left, right, (((1,), (1,)), ((), ())), preferred_element_...  54.3 us
    dot_general x21, matrix products, token_sum(): lax.dot_general(left, right, (((0,), (0,)), ((), ())), preferred_element_...  40.1 us
    dot_general x21, matrix products, dot(): lax.dot_general(left, right, (((1,), (0,)), ((), ())), preferred_element_...  35.9 us
    all_to_all x1, starting transfers between devices, local(): lax.all_to_all(jnp.concatenate([pieces, marks], axis=2), SEQ, 0, 0, tiled...  19.6 us
    ppermute x7, starting transfers between devices, swap_heads(): return lax.ppermute(array, HEAD, SWAP)  17.5 us
  transfers between devices with their start and end apart: 13, of which 9 were waited for; matrix products, arithmetic and copies ran while one was open for 10% of the time, Pallas kernels for 0%

profile of v1, /device:TPU:0, one launch (start us, length us, event | category | flops | bytes accessed | tf_op | source)
XLA Modules:
  0.0 581.7 jit_solution(3090535731447940010)
XLA Ops:
  17.8 4.4 fusion.126
  25.4 19.6 %all-to-all-start = ((bf16[64,8,512]{2,1,0:T(8,128)(2,1)}), bf16[64,8,512]{2,1,0:T(8,128)(2,1)}, u32[]{:S(2)}, u32[]{:S(2)}) async-start(bf16[64,8,512]{2,1,0:T(8,128)(2,1)} %pad_maximum_fusion.3), calls=%async_computation | async-start | bytes 1048576 | tf_op jit(solution)/shard_map/all_to_all | solution.py:153
  49.0 8.2 %all-to-all-done = bf16[64,8,512]{2,1,0:T(8,128)(2,1)} async-done(((bf16[64,8,512]{2,1,0:T(8,128)(2,1)}), bf16[64,8,512]{2,1,0:T(8,128)(2,1)}, u32[]{:S(2)}, u32[]{:S(2)}) %all-to-all-start) | async-done | bytes 524320 | tf_op jit(solution)/shard_map/all_to_all | solution.py:153
  61.5 5.5 all-to-all-start.1
  70.7 8.7 %all-to-all-done.1 = bf16[64,8,432]{2,1,0:T(8,128)(2,1)} async-done(((bf16[64,8,432]{2,1,0:T(8,128)(2,1)}), bf16[64,8,432]{2,1,0:T(8,128)(2,1)}, u32[]{:S(2)}, u32[]{:S(2)}) %all-to-all-start.1) | async-done | bytes 442400 | tf_op jit(solution)/shard_map/all_to_all | solution.py:161
  99.2 59.8 %collective-permute-done.2 = bf16[896,512]{1,0:T(8,128)(2,1)} collective-permute-done((bf16[896,512]{1,0:T(8,128)(2,1)}, bf16[896,512]{1,0:T(8,128)(2,1)}, u32[]{:S(2)}, u32[]{:S(2)}) %collective-permute-start.2) | collective-permute-done | bytes 917536 | tf_op jit(solution)/shard_map/ppermute | solution.py:44
  171.6 5.5 multiply_convert_fusion.4
  186.2 5.3 convolution_convert_fusion.1
  197.9 28.3 %collective-permute-done.3 = bf16[896,1024]{1,0:T(8,128)(2,1)} collective-permute-done((bf16[896,1024]{1,0:T(8,128)(2,1)}, bf16[896,1024]{1,0:T(8,128)(2,1)}, u32[]{:S(2)}, u32[]{:S(2)}) %collective-permute-start.3) | collective-permute-done | bytes 1835040 | tf_op jit(solution)/shard_map/ppermute | solution.py:44
  226.2 3.8 multiply_reduce_fusion
  230.1 4.5 fusion.172
  257.0 5.9 %all-to-all-start.2 = ((bf16[64,8,432]{2,1,0:T(8,128)(2,1)}), bf16[64,8,432]{2,1,0:T(8,128)(2,1)}, u32[]{:S(2)}, u32[]{:S(2)}) async-start(bf16[64,8,432]{2,1,0:T(8,128)(2,1)} %bitcast.138), calls=%async_computation.2 | async-start | bytes 1048576 | tf_op jit(solution)/shard_map/all_to_all | solution.py:231
  262.9 3.9 convolution_convert_fusion.6
  280.0 9.2 %all-to-all-start.3 = ((bf16[64,8,432]{2,1,0:T(8,128)(2,1)}), bf16[64,8,432]{2,1,0:T(8,128)(2,1)}, u32[]{:S(2)}, u32[]{:S(2)}) async-start(bf16[64,8,432]{2,1,0:T(8,128)(2,1)} %copy.72), calls=%async_computation.3 | async-start | bytes 1048576 | tf_op jit(solution)/shard_map/all_to_all | solution.py:235
  295.1 6.5 %all-to-all-done.3 = bf16[64,8,432]{2,1,0:T(8,128)(2,1)} async-done(((bf16[64,8,432]{2,1,0:T(8,128)(2,1)}), bf16[64,8,432]{2,1,0:T(8,128)(2,1)}, u32[]{:S(2)}, u32[]{:S(2)}) %all-to-all-start.3) | async-done | bytes 442400 | tf_op jit(solution)/shard_map/all_to_all | solution.py:235
  324.7 7.3 %add_convert_fusion = bf16[896,1024]{1,0:T(8,128)(2,1)S(1)} fusion(f32[896,1024]{1,0:T(8,128)} %fusion.43, f32[896,1024]{1,0:T(8,128)S(1)} %fusion.93, f32[896,1024]{1,0:T(8,128)S(1)} %fusion.89, f32[896,1024]{1,0:T(8,128)} %fusion.49, f32[896,1024]{1,0:T(8,128)} %fusion.46, f32[896,1024]{1,0:T(8,128)S(1)} %fusion.101, f32[896,1024]{1,0:T(8,128)S(1)} %fusion.97, ...), kind=kOutput, calls=%fused_computation.13 | convolution fusion | flops 800063488 | bytes 29184000 | tf_op jit(solution)/shard_map/dot_general | solution.py:26
  342.5 13.8 %collective-permute-done.4 = bf16[896,512]{1,0:T(8,128)(2,1)S(1)} collective-permute-done((bf16[896,512]{1,0:T(8,128)(2,1)S(1)}, bf16[896,512]{1,0:T(8,128)(2,1)S(1)}, u32[]{:S(2)}, u32[]{:S(2)}) %collective-permute-start.4) | collective-permute-done | bytes 917536 | tf_op jit(solution)/shard_map/ppermute | solution.py:44
  364.0 66.2 %concatenate.84 = bf16[1024,6216]{0,1:T(8,128)(2,1)} concatenate(bf16[1024,256]{0,1:T(8,128)(2,1)} %convolution_convert_fusion.15, bf16[1024,256]{0,1:T(8,128)(2,1)} %convolution_convert_fusion.14, bf16[1024,256]{0,1:T(8,128)(2,1)} %convolution_convert_fusion.13, bf16[1024,256]{0,1:T(8,128)(2,1)} %convolution_convert_fusion.12, bf16[1024,432]{0,1:T(8,128)(2,1)} %convolution_convert_fusion.9, ...), dimensions={1} | concatenate | bytes 25460736 | tf_op jit(solution)/shard_map/concatenate | solution.py:296
  430.3 16.1 %copy.73 = bf16[1024,6216]{1,0:T(8,128)(2,1)} copy(bf16[1024,6216]{0,1:T(8,128)(2,1)} %concatenate.84) | data formatting | bytes 25460736 | tf_op jit(solution)/shard_map/concatenate | solution.py:296
  446.4 8.0 %select_bitcast_fusion = bf16[32,16,6216]{2,1,0:T(8,128)(2,1)} fusion(pred[]{:T(512)S(6)} %eq.52, bf16[32,2,16,6216]{3,2,1,0:T(8,128)(2,1)} %bitcast.136), kind=kLoop, calls=%fused_computation.3 | loop fusion | flops 3182592 | bytes 19095552 | tf_op jit(solution)/shard_map/jit(_where)/select_n | solution.py:299
  454.4 10.6 %collective-permute-done.7 = bf16[32,16,6216]{2,1,0:T(8,128)(2,1)S(1)} collective-permute-done((bf16[32,16,6216]{2,1,0:T(8,128)(2,1)}, bf16[32,16,6216]{2,1,0:T(8,128)(2,1)S(1)}, u32[]{:S(2)}, u32[]{:S(2)}) %collective-permute-start.7) | collective-permute-done | bytes 6365216 | tf_op jit(solution)/shard_map/ppermute | solution.py:300
  464.9 9.2 %fusion = bf16[32,16,6216]{2,1,0:T(8,128)(2,1)} fusion(bf16[32,16,6216]{2,1,0:T(8,128)(2,1)S(1)} %collective-permute-done.7, pred[]{:T(512)S(6)} %eq.52, bf16[32,2,16,6216]{3,2,1,0:T(8,128)(2,1)} %bitcast.137), kind=kLoop, calls=%fused_computation.1 | loop fusion | flops 15912960 | bytes 25460736 | tf_op jit(solution)/shard_map/convert_element_type | solution.py:301
  474.1 4.9 all-to-all-start.4
  486.7 84.7 %collective-permute-done.1 = bf16[896,512]{1,0:T(8,128)(2,1)S(1)} collective-permute-done((bf16[896,512]{1,0:T(8,128)(2,1)S(1)}, bf16[896,512]{1,0:T(8,128)(2,1)S(1)}, u32[]{:S(2)}, u32[]{:S(2)}) %collective-permute-start.1) | collective-permute-done | bytes 917536 | tf_op jit(solution)/shard_map/ppermute | solution.py:44
  (356 shorter events, 179.7 us)
Async XLA Ops:
  0.6 170.9 %copy-start = (bf16[864,1024]{1,0:T(8,128)(2,1)S(1)}, bf16[864,1024]{1,0:T(8,128)(2,1)}, u32[]{:S(2)}) copy-start(bf16[864,1024]{1,0:T(8,128)(2,1)} %param.30) | copy-start | bytes 5308420
  25.4 31.7 %all-to-all-start = ((bf16[64,8,512]{2,1,0:T(8,128)(2,1)}), bf16[64,8,512]{2,1,0:T(8,128)(2,1)}, u32[]{:S(2)}, u32[]{:S(2)}) async-start(bf16[64,8,512]{2,1,0:T(8,128)(2,1)} %pad_maximum_fusion.3), calls=%async_computation | async-start | bytes 1048576 | tf_op jit(solution)/shard_map/all_to_all | solution.py:153
  49.0 32.1 %copy-start.16 = (bf16[896,896]{1,0:T(8,128)(2,1)}, bf16[896,896]{1,0:T(8,128)(2,1)S(1)}, u32[]{:S(2)}) copy-start(bf16[896,896]{1,0:T(8,128)(2,1)S(1)} %multiply_convert_fusion.3) | copy-start | bytes 4816900
  61.5 17.9 %all-to-all-start.1 = ((bf16[64,8,432]{2,1,0:T(8,128)(2,1)}), bf16[64,8,432]{2,1,0:T(8,128)(2,1)}, u32[]{:S(2)}, u32[]{:S(2)}) async-start(bf16[64,8,432]{2,1,0:T(8,128)(2,1)} %copy.68), calls=%async_computation.1 | async-start | bytes 1048576 | tf_op jit(solution)/shard_map/all_to_all | solution.py:161
  95.2 65.4 %collective-permute-start = (bf16[896,1024]{1,0:T(8,128)(2,1)}, bf16[896,1024]{1,0:T(8,128)(2,1)}, u32[]{:S(2)}, u32[]{:S(2)}) collective-permute-start(bf16[896,1024]{1,0:T(8,128)(2,1)} %add_convert_fusion.3), channel_id=1, source_target_pairs={{0,1},{1,0},{2,3},{3,2},{4,5},{5,4},{6,7},{7,6},{8,9},{9,8},{10,11... | collective-permute-start | bytes 5505032 | tf_op jit(solution)/shard_map/ppermute | solution.py:44
  98.8 60.2 %collective-permute-start.2 = (bf16[896,512]{1,0:T(8,128)(2,1)}, bf16[896,512]{1,0:T(8,128)(2,1)}, u32[]{:S(2)}, u32[]{:S(2)}) collective-permute-start(bf16[896,512]{1,0:T(8,128)(2,1)} %param.31), channel_id=1, source_target_pairs={{0,1},{1,0},{2,3},{3,2},{4,5},{5,4},{6,7},{7,6},{8,9},{9,8},{10,11... | collective-permute-start | bytes 2752520 | tf_op jit(solution)/shard_map/ppermute | solution.py:44
  99.2 61.4 %copy-start.9 = (bf16[896,1024]{1,0:T(8,128)(2,1)S(1)}, bf16[896,1024]{1,0:T(8,128)(2,1)}, u32[]{:S(2)}) copy-start(bf16[896,1024]{1,0:T(8,128)(2,1)} %param.16) | copy-start | bytes 5505028
  182.8 43.4 %collective-permute-start.3 = (bf16[896,1024]{1,0:T(8,128)(2,1)}, bf16[896,1024]{1,0:T(8,128)(2,1)}, u32[]{:S(2)}, u32[]{:S(2)}) collective-permute-start(bf16[896,1024]{1,0:T(8,128)(2,1)} %add_convert_fusion.1), channel_id=1, source_target_pairs={{0,1},{1,0},{2,3},{3,2},{4,5},{5,4},{6,7},{7,6},{8,9},{9,8},{10,11... | collective-permute-start | bytes 5505032 | tf_op jit(solution)/shard_map/ppermute | solution.py:44
  194.7 31.5 %copy-start.2 = (f32[896,1024]{1,0:T(8,128)S(1)}, f32[896,1024]{1,0:T(8,128)}, u32[]{:S(2)}) copy-start(f32[896,1024]{1,0:T(8,128)} %copy-done.1) | copy-start | bytes 11010052
  197.9 32.2 %copy-start.36 = (bf16[896,512]{1,0:T(8,128)(2,1)S(1)}, bf16[896,512]{1,0:T(8,128)(2,1)}, u32[]{:S(2)}) copy-start(bf16[896,512]{1,0:T(8,128)(2,1)} %copy-done.35) | copy-start | bytes 2752516
  197.9 32.2 %copy-start.38 = (bf16[896,512]{1,0:T(8,128)(2,1)S(1)}, bf16[896,512]{1,0:T(8,128)(2,1)}, u32[]{:S(2)}) copy-start(bf16[896,512]{1,0:T(8,128)(2,1)} %copy-done.37) | copy-start | bytes 2752516
  257.0 20.6 %all-to-all-start.2 = ((bf16[64,8,432]{2,1,0:T(8,128)(2,1)}), bf16[64,8,432]{2,1,0:T(8,128)(2,1)}, u32[]{:S(2)}, u32[]{:S(2)}) async-start(bf16[64,8,432]{2,1,0:T(8,128)(2,1)} %bitcast.138), calls=%async_computation.2 | async-start | bytes 1048576 | tf_op jit(solution)/shard_map/all_to_all | solution.py:231
  280.0 21.6 %all-to-all-start.3 = ((bf16[64,8,432]{2,1,0:T(8,128)(2,1)}), bf16[64,8,432]{2,1,0:T(8,128)(2,1)}, u32[]{:S(2)}, u32[]{:S(2)}) async-start(bf16[64,8,432]{2,1,0:T(8,128)(2,1)} %copy.72), calls=%async_computation.3 | async-start | bytes 1048576 | tf_op jit(solution)/shard_map/all_to_all | solution.py:235
  307.4 16.6 %copy-start.62 = (bf16[896,128]{0,1:T(8,128)(2,1)}, bf16[896,128]{0,1:T(8,128)(2,1)S(1)}, u32[]{:S(2)}) copy-start(bf16[896,128]{0,1:T(8,128)(2,1)S(1)} %get-tuple-element.87) | copy-start | bytes 688132
  332.2 24.1 %collective-permute-start.4 = (bf16[896,512]{1,0:T(8,128)(2,1)S(1)}, bf16[896,512]{1,0:T(8,128)(2,1)S(1)}, u32[]{:S(2)}, u32[]{:S(2)}) collective-permute-start(bf16[896,512]{1,0:T(8,128)(2,1)S(1)} %broadcast_select_fusion), channel_id=1, source_target_pairs={{0,1},{1,0},{2,3},{3,2},{4,5},{5,4},{6,7},{7,6},{8,9},{9,8},{10,11... | collective-permute-start | bytes 2752520 | tf_op jit(solution)/shard_map/ppermute | solution.py:44
  358.8 5.2 collective-permute-start.6
  454.4 10.6 %collective-permute-start.7 = (bf16[32,16,6216]{2,1,0:T(8,128)(2,1)}, bf16[32,16,6216]{2,1,0:T(8,128)(2,1)S(1)}, u32[]{:S(2)}, u32[]{:S(2)}) collective-permute-start(bf16[32,16,6216]{2,1,0:T(8,128)(2,1)} %select_bitcast_fusion), channel_id=1, source_target_pairs={{0,2},{2,0},{1,3},{3,1},{4,6},{6,4},{5,7},{7,5},{8,10},{10,8},{9,1... | collective-permute-start | bytes 19095560 | tf_op jit(solution)/shard_map/ppermute | solution.py:300
  474.1 101.4 %all-to-all-start.4 = ((bf16[32,16,6216]{2,1,0:T(8,128)(2,1)}), bf16[32,16,6216]{2,1,0:T(8,128)(2,1)}, u32[]{:S(2)}, u32[]{:S(2)}) async-start(bf16[32,16,6216]{2,1,0:T(8,128)(2,1)} %fusion), calls=%async_computation.4 | async-start | bytes 12845056 | tf_op jit(solution)/shard_map/all_to_all | solution.py:302
  479.0 92.4 %copy-start.3 = (f32[896,1024]{1,0:T(8,128)S(1)}, f32[896,1024]{1,0:T(8,128)}, u32[]{:S(2)}) copy-start(f32[896,1024]{1,0:T(8,128)} %copy-done.1) | copy-start | bytes 11010052
  482.8 88.7 %collective-permute-start.1 = (bf16[896,512]{1,0:T(8,128)(2,1)S(1)}, bf16[896,512]{1,0:T(8,128)(2,1)S(1)}, u32[]{:S(2)}, u32[]{:S(2)}) collective-permute-start(bf16[896,512]{1,0:T(8,128)(2,1)S(1)} %broadcast_select_fusion.4), channel_id=1, source_target_pairs={{0,1},{1,0},{2,3},{3,2},{4,5},{5,4},{6,7},{7,6},{8,9},{9,8},{10,11... | collective-permute-start | bytes 2752520 | tf_op jit(solution)/shard_map/ppermute | solution.py:44
  485.8 87.3 %copy-start.14 = (f32[896,512]{1,0:T(8,128)S(1)}, f32[896,512]{1,0:T(8,128)}, u32[]{:S(2)}) copy-start(f32[896,512]{1,0:T(8,128)} %get-tuple-element.41) | copy-start | bytes 5505028
  485.8 87.3 %copy-start.30 = (bf16[896,512]{1,0:T(8,128)(2,1)S(1)}, bf16[896,512]{1,0:T(8,128)(2,1)}, u32[]{:S(2)}) copy-start(bf16[896,512]{1,0:T(8,128)(2,1)} %get-tuple-element.40) | copy-start | bytes 2752516
  485.8 87.3 %copy-start.73 = (f32[896]{0:T(1024)S(1)}, f32[896]{0:T(1024)}, u32[]{:S(2)}) copy-start(f32[896]{0:T(1024)} %copy-done.72) | copy-start | bytes 10756
  485.8 87.2 %collective-permute-start.5 = (f32[2,896]{1,0:T(2,128)S(1)}, f32[2,896]{1,0:T(2,128)S(1)}, u32[]{:S(2)}, u32[]{:S(2)}) collective-permute-start(f32[2,896]{1,0:T(2,128)S(1)} %pad_maximum_fusion.15), channel_id=1, source_target_pairs={{0,1},{1,0},{2,3},{3,2},{4,5},{5,4},{6,7},{7,6},{8,9},{9,8},{10,11... | collective-permute-start | bytes 21512 | tf_op jit(solution)/shard_map/ppermute | solution.py:44
  (87 other events, 277.2 us)

commit v2 on v1

--- a/solution.py
+++ b/solution.py
@@ -55,6 +55,16 @@
     second = rest.astype(bf16)
     third = (rest - second.astype(f32)).astype(bf16)
     return first, second, third
+
+
+def exchange_sum(grads):
+    blocks = lax.axis_size(SEQ)
+    rows = grads[0].shape[0] // blocks
+    stacked = jnp.concatenate([g.astype(bf16).reshape(blocks, 1, rows, -1) for g in grads], axis=1)
+    stacked = stacked.reshape(blocks, len(grads) * rows, -1)
+    shares = lax.all_to_all(stacked, SEQ, 0, 0, tiled=True)
+    total = jnp.sum(shares.astype(f32), axis=0)
+    return jnp.swapaxes(total.reshape(len(grads), rows, -1), 0, 1)
 
 
 def block_weights(log_totals, starts, row_count, head):
@@ -100,7 +110,6 @@
     blocks = lax.axis_size(SEQ)
     seq_at = lax.axis_index(SEQ)
     head_at = lax.axis_index(HEAD)
-    core_at = lax.axis_index("core")
     first_head = head_at == 0
     block_start = seq_at * rows
     key_scale = dk ** (-0.5)
@@ -159,6 +168,7 @@
         carried, arrived[:, :, :dv], (((1,), (0,)), ((), ())), preferred_element_type=f32
     ).astype(bf16)
     incoming = lax.all_to_all(summed, SEQ, 0, 0, tiled=True).reshape(heads * dk, dv)
+    incoming, other_cot = lax.optimization_barrier((incoming, other_cot))
 
     mixed, ghats, ginvs, weights = [], [], [], []
     branch = None
@@ -193,9 +203,6 @@
     low, high = ffn_out[:, :half], ffn_out[:, half:]
     arrived_out = swap_heads(jnp.where(first_head, high, low))
     own_resid = jnp.where(first_head, resid[:, :half], resid[:, half:])
-    output = (
-        own_resid + (jnp.where(first_head, low, high).astype(f32) + arrived_out.astype(f32))
-    ).astype(bf16)
 
     cot = jnp.concatenate(
         [
@@ -214,6 +221,14 @@
     bias2_grad = jnp.sum(normed2_grad, axis=0)
     resid_grad = cot.astype(f32) + norm_back(xhat2, inverse2, normed2_grad * norm2_gain)
     branch_grad = resid_grad.astype(bf16)
+
+    ffn_sum = exchange_sum(
+        [
+            token_sum(normed2, gate_ff_grad),
+            token_sum(normed2, up_ff_grad),
+            token_sum(cot, hidden),
+        ]
+    )
 
     gate_grads, retained_grads, state_parts = [], [], []
     for h in range(heads):
@@ -233,6 +248,18 @@
         carried, arrived_back, (((0,), (0,)), ((), ())), preferred_element_type=f32
     ).astype(bf16)
     outgoing = lax.all_to_all(summed_back, SEQ, 0, 0, tiled=True).reshape(heads * dk, dv)
+
+    gate_grad = jnp.concatenate(gate_grads, axis=1)
+    branch_sum = exchange_sum(
+        [
+            token_sum(normed1, gate_grad),
+            token_sum(branch_grad, jnp.concatenate(mixed, axis=1)),
+        ]
+    )
+    outgoing, arrived_out = lax.optimization_barrier((outgoing, arrived_out))
+    output = (
+        own_resid + (jnp.where(first_head, low, high).astype(f32) + arrived_out.astype(f32))
+    ).astype(bf16)
 
     query_grads, key_grads, value_grads = [], [], []
     for h in range(heads):
@@ -283,35 +310,34 @@
     vector_high = vectors.astype(bf16)
     vector_low = (vectors - vector_high.astype(f32)).astype(bf16)
 
-    grads = [token_sum(normed1, query_grads[h]).astype(bf16) for h in range(heads)]
-    grads += [token_sum(normed1, key_grads[h]).astype(bf16) for h in range(heads)]
-    grads += [token_sum(normed1, value_grads[h]).astype(bf16) for h in range(heads)]
-    grads += [token_sum(normed1, gate_grads[h]).astype(bf16) for h in range(heads)]
-    grads += [token_sum(branch_grad, mixed[h]).astype(bf16) for h in range(heads)]
-    grads += [token_sum(normed2, gate_ff_grad).astype(bf16)]
-    grads += [token_sum(normed2, up_ff_grad).astype(bf16)]
-    grads += [token_sum(cot, hidden).astype(bf16)]
-    grads += [vector_high.T, vector_low.T]
-    widths = [g.shape[1] for g in grads]
-    everything = jnp.concatenate(grads, axis=1)
-    everything = everything.reshape(blocks // 2, 2, width // blocks, -1)
-    kept = jnp.where(core_at == 0, everything[:, 0], everything[:, 1])
-    sent = jnp.where(core_at == 0, everything[:, 1], everything[:, 0])
-    got = lax.ppermute(sent, "core", SWAP)
-    chip_sum = (kept.astype(f32) + got.astype(f32)).astype(bf16)
-    shares = lax.all_to_all(chip_sum, CHIPS, 0, 0, tiled=True)
-    whole = jnp.sum(shares.astype(f32), axis=0)
-    parts, at = [], 0
-    for wide_part in widths:
-        parts.append(whole[:, at : at + wide_part])
-        at += wide_part
-    query_out = jnp.concatenate(parts[0:2], axis=1)
-    key_out = jnp.concatenate(parts[2:4], axis=1)
-    value_out = jnp.concatenate(parts[4:6], axis=1)
-    gate_out = jnp.concatenate(parts[6:8], axis=1)
-    output_out = jnp.concatenate(parts[8:10], axis=1).T
-    ffn_gate_out, ffn_up_out, ffn_down_out = parts[10], parts[11], parts[12].T
-    vector_out = parts[13] + parts[14]
+    query_grad = jnp.concatenate(query_grads, axis=1)
+    key_grad = jnp.concatenate(key_grads, axis=1)
+    value_grad = jnp.concatenate(value_grads, axis=1)
+    marks = jnp.concatenate([vector_high, vector_low], axis=0).T
+    spare = 128 - value_grad.shape[1] % 128
+    value_part = jnp.pad(token_sum(normed1, value_grad), ((0, 0), (0, spare)))
+    value_part = value_part.astype(bf16) + jnp.pad(
+        marks, ((0, 0), (value_grad.shape[1], spare - marks.shape[1]))
+    )
+    projection_sum = exchange_sum(
+        [
+            jnp.concatenate(
+                [
+                    token_sum(normed1, query_grad).astype(bf16),
+                    token_sum(normed1, key_grad).astype(bf16),
+                    value_part,
+                ],
+                axis=1,
+            )
+        ]
+    )[:, 0]
+    query_out = projection_sum[:, : heads * dk]
+    key_out = projection_sum[:, heads * dk : 2 * heads * dk]
+    value_out = projection_sum[:, 2 * heads * dk : heads * (2 * dk + dv)]
+    marks_out = projection_sum[:, heads * (2 * dk + dv) :]
+    vector_out = marks_out[:, :4] + marks_out[:, 4:8]
+    gate_out, output_out = branch_sum[:, 0], branch_sum[:, 1].T
+    ffn_gate_out, ffn_up_out, ffn_down_out = ffn_sum[:, 0], ffn_sum[:, 1], ffn_sum[:, 2].T
     return (
         output,
         input_grad,

time: 593 us -> 512 us (0.86)
  the two profiles are of different devices: /device:TPU:0 before, /device:TPU:21 now
where the time goes in v2:
time: 512 us; the launch traced here: 502 us
  waiting for transfers between devices  166 us (32%)
  matrix products  135 us (26%)
  starting transfers between devices  86.1 us (17%)
  other arithmetic  59.7 us (12%)
  local copies, waits for them, and re-layouts  52.8 us (10%)
    ppermute x7, waiting for transfers between devices, swap_heads(): return lax.ppermute(array, HEAD, SWAP)  137 us
    dot_general x21, matrix products, row_times(): lax.dot_general(left, right, (((1,), (1,)), ((), ())), preferred_element_...  61.4 us
    dot_general x21, matrix products, dot(): lax.dot_general(left, right, (((1,), (0,)), ((), ())), preferred_element_...  44.1 us
    all_to_all x3, starting transfers between devices, exchange_sum(): shares = lax.all_to_all(stacked, SEQ, 0, 0, tiled=True)  31 us
    dot_general x16, matrix products, token_sum(): lax.dot_general(left, right, (((0,), (0,)), ((), ())), preferred_element_...  27.5 us
    all_to_all x3, waiting for transfers between devices, exchange_sum(): shares = lax.all_to_all(stacked, SEQ, 0, 0, tiled=True)  24.9 us
    convert_element_type x5, local copies, waits for them, and re-layouts, exchange_sum(): g.astype(bf16).reshape(blocks, 1, rows, -1)  16.4 us
    unnamed x280, local copies, waits for them, and re-layouts  15.1 us
  transfers between devices with their start and end apart: 14, of which 7 were waited for; matrix products, arithmetic and copies ran while one was open for 38% of the time, Pallas kernels for 0%

profile of v2, /device:TPU:21, one launch (start us, length us, event | category | flops | bytes accessed | tf_op | source)
XLA Modules:
  0.0 502.0 jit_solution(826687613242627288)
XLA Ops:
  22.2 4.3 fusion.144
  32.1 9.2 %all-to-all-start = ((bf16[64,8,512]{2,1,0:T(8,128)(2,1)}), bf16[64,8,512]{2,1,0:T(8,128)(2,1)S(1)}, u32[]{:S(2)}, u32[]{:S(2)}) async-start(bf16[64,8,512]{2,1,0:T(8,128)(2,1)} %pad_maximum_fusion.6), calls=%async_computation | async-start | bytes 1048576 | tf_op jit(solution)/shard_map/all_to_all | solution.py:162
  52.7 8.8 %all-to-all-start.1 = ((bf16[64,8,432]{2,1,0:T(8,128)(2,1)}), bf16[64,8,432]{2,1,0:T(8,128)(2,1)S(1)}, u32[]{:S(2)}, u32[]{:S(2)}) async-start(bf16[64,8,432]{2,1,0:T(8,128)(2,1)} %copy.81), calls=%async_computation.1 | async-start | bytes 1048576 | tf_op jit(solution)/shard_map/all_to_all | solution.py:170
  61.7 4.0 fusion.201
  65.6 4.3 all-to-all-done.1
  88.8 37.8 %collective-permute-done.1 = bf16[896,1024]{1,0:T(8,128)(2,1)} collective-permute-done((bf16[896,1024]{1,0:T(8,128)(2,1)}, bf16[896,1024]{1,0:T(8,128)(2,1)}, u32[]{:S(2)}, u32[]{:S(2)}) %collective-permute-start.1) | collective-permute-done | bytes 1835040 | tf_op jit(solution)/shard_map/ppermute | solution.py:44
  134.8 4.6 multiply_convert_fusion.5
  143.8 3.8 copy.92
  147.6 4.2 fusion.203
  167.3 4.0 convolution_convert_fusion.3
  180.3 17.0 %collective-permute-done.2 = bf16[896,1024]{1,0:T(8,128)(2,1)} collective-permute-done((bf16[896,1024]{1,0:T(8,128)(2,1)}, bf16[896,1024]{1,0:T(8,128)(2,1)}, u32[]{:S(2)}, u32[]{:S(2)}) %collective-permute-start.2) | collective-permute-done | bytes 1835040 | tf_op jit(solution)/shard_map/ppermute | solution.py:44
  197.3 3.8 multiply_reduce_fusion
  227.0 13.5 %all-to-all-start.2 = ((bf16[64,8,432]{2,1,0:T(8,128)(2,1)}), bf16[64,8,432]{2,1,0:T(8,128)(2,1)}, u32[]{:S(2)}, u32[]{:S(2)}) async-start(bf16[64,8,432]{2,1,0:T(8,128)(2,1)} %bitcast.139), calls=%async_computation.2 | async-start | bytes 1048576 | tf_op jit(solution)/shard_map/all_to_all | solution.py:246
  251.9 9.0 %all-to-all-start.3 = ((bf16[64,8,432]{2,1,0:T(8,128)(2,1)}), bf16[64,8,432]{2,1,0:T(8,128)(2,1)}, u32[]{:S(2)}, u32[]{:S(2)}) async-start(bf16[64,8,432]{2,1,0:T(8,128)(2,1)} %copy.85), calls=%async_computation.3 | async-start | bytes 1048576 | tf_op jit(solution)/shard_map/all_to_all | solution.py:250
  267.4 3.9 copy.87
  273.7 9.4 %all-to-all-start.6 = ((bf16[64,48,864]{2,1,0:T(8,128)(2,1)}), bf16[64,48,864]{2,1,0:T(8,128)(2,1)}, u32[]{:S(2)}, u32[]{:S(2)}) async-start(bf16[64,48,864]{2,1,0:T(8,128)(2,1)} %bitcast.126), calls=%async_computation.6 | async-start | bytes 11010048 | tf_op jit(solution)/shard_map/all_to_all | solution.py:65
  321.5 24.9 %all-to-all-done.6 = bf16[64,48,864]{2,1,0:T(8,128)(2,1)} async-done(((bf16[64,48,864]{2,1,0:T(8,128)(2,1)}), bf16[64,48,864]{2,1,0:T(8,128)(2,1)}, u32[]{:S(2)}, u32[]{:S(2)}) %all-to-all-start.6) | async-done | bytes 5308448 | tf_op jit(solution)/shard_map/all_to_all | solution.py:65
  346.4 11.3 %all-to-all-start.5 = ((bf16[64,32,864]{2,1,0:T(8,128)(2,1)}), bf16[64,32,864]{2,1,0:T(8,128)(2,1)}, u32[]{:S(2)}, u32[]{:S(2)}) async-start(bf16[64,32,864]{2,1,0:T(8,128)(2,1)} %bitcast.128), calls=%async_computation.5 | async-start | bytes 7340032 | tf_op jit(solution)/shard_map/all_to_all | solution.py:65
  357.7 10.6 %add_convert_fusion = bf16[896,1024]{1,0:T(8,128)(2,1)S(1)} fusion(f32[896,1024]{1,0:T(8,128)} %fusion.61, f32[896,1024]{1,0:T(8,128)} %fusion.111, f32[896,1024]{1,0:T(8,128)} %fusion.107, f32[896,1024]{1,0:T(8,128)} %fusion.67, f32[896,1024]{1,0:T(8,128)} %fusion.64, f32[896,1024]{1,0:T(8,128)} %fusion.119, f32[896,1024]{1,0:T(8,128)} %fusion.115, ...), kind=kOutput, calls=%fused_computation.15 | convolution fusion | flops 800063488 | bytes 29184000 | tf_op jit(solution)/shard_map/dot_general | solution.py:26
  373.2 44.9 %collective-permute-done.4 = bf16[896,512]{1,0:T(8,128)(2,1)S(1)} collective-permute-done((bf16[896,512]{1,0:T(8,128)(2,1)S(1)}, bf16[896,512]{1,0:T(8,128)(2,1)S(1)}, u32[]{:S(2)}, u32[]{:S(2)}) %collective-permute-start.4) | collective-permute-done | bytes 917536 | tf_op jit(solution)/shard_map/ppermute | solution.py:44
  426.8 6.3 %copy.86 = bf16[1024,1920]{1,0:T(8,128)(2,1)} copy(bf16[1024,1920]{0,1:T(8,128)(2,1)} %pad_maximum_fusion.1) | data formatting | bytes 7864320 | tf_op jit(solution)/shard_map/concatenate | solution.py:324
  433.1 10.3 %all-to-all-start.4 = ((bf16[64,16,1920]{2,1,0:T(8,128)(2,1)}), bf16[64,16,1920]{2,1,0:T(8,128)(2,1)}, u32[]{:S(2)}, u32[]{:S(2)}) async-start(bf16[64,16,1920]{2,1,0:T(8,128)(2,1)} %bitcast.127), calls=%async_computation.4 | async-start | bytes 7864320 | tf_op jit(solution)/shard_map/all_to_all | solution.py:65
  446.8 4.6 fusion.18
  451.4 36.3 %collective-permute-done.5 = f32[2,896]{1,0:T(2,128)S(1)} collective-permute-done((f32[2,896]{1,0:T(2,128)S(1)}, f32[2,896]{1,0:T(2,128)S(1)}, u32[]{:S(2)}, u32[]{:S(2)}) %collective-permute-start.5) | collective-permute-done | bytes 7200 | tf_op jit(solution)/shard_map/ppermute | solution.py:44
  (452 shorter events, 208.5 us)
Async XLA Ops:
  0.6 134.1 %copy-start = (bf16[1024,864]{0,1:T(8,128)(2,1)S(1)}, bf16[1024,864]{0,1:T(8,128)(2,1)}, u32[]{:S(2)}) copy-start(bf16[1024,864]{0,1:T(8,128)(2,1)} %param.29) | copy-start | bytes 5308420
  0.7 65.0 %collective-permute-start = (bf16[896,512]{1,0:T(8,128)(2,1)}, bf16[896,512]{1,0:T(8,128)(2,1)}, u32[]{:S(2)}, u32[]{:S(2)}) collective-permute-start(bf16[896,512]{1,0:T(8,128)(2,1)} %param.31), channel_id=1, source_target_pairs={{0,1},{1,0},{2,3},{3,2},{4,5},{5,4},{6,7},{7,6},{8,9},{9,8},{10,11... | collective-permute-start | bytes 2752520 | tf_op jit(solution)/shard_map/ppermute | solution.py:44
  19.5 28.1 %copy-start.105 = (s32[896]{0:T(1024)}, s32[896]{0:T(1024)S(1)}, u32[]{:S(2)}) copy-start(s32[896]{0:T(1024)S(1)} %get-tuple-element.115) | copy-start | bytes 10756
  26.6 193.9 %copy-start.43 = (bf16[896,128]{0,1:T(8,128)(2,1)}, bf16[896,128]{0,1:T(8,128)(2,1)S(1)}, u32[]{:S(2)}) copy-start(bf16[896,128]{0,1:T(8,128)(2,1)S(1)} %get-tuple-element.73) | copy-start | bytes 688132
  32.1 18.2 %all-to-all-start = ((bf16[64,8,512]{2,1,0:T(8,128)(2,1)}), bf16[64,8,512]{2,1,0:T(8,128)(2,1)S(1)}, u32[]{:S(2)}, u32[]{:S(2)}) async-start(bf16[64,8,512]{2,1,0:T(8,128)(2,1)} %pad_maximum_fusion.6), calls=%async_computation | async-start | bytes 1048576 | tf_op jit(solution)/shard_map/all_to_all | solution.py:162
  52.7 17.2 %all-to-all-start.1 = ((bf16[64,8,432]{2,1,0:T(8,128)(2,1)}), bf16[64,8,432]{2,1,0:T(8,128)(2,1)S(1)}, u32[]{:S(2)}, u32[]{:S(2)}) async-start(bf16[64,8,432]{2,1,0:T(8,128)(2,1)} %copy.81), calls=%async_computation.1 | async-start | bytes 1048576 | tf_op jit(solution)/shard_map/all_to_all | solution.py:170
  83.4 43.2 %collective-permute-start.1 = (bf16[896,1024]{1,0:T(8,128)(2,1)}, bf16[896,1024]{1,0:T(8,128)(2,1)}, u32[]{:S(2)}, u32[]{:S(2)}) collective-permute-start(bf16[896,1024]{1,0:T(8,128)(2,1)} %add_convert_fusion.3), channel_id=1, source_target_pairs={{0,1},{1,0},{2,3},{3,2},{4,5},{5,4},{6,7},{7,6},{8,9},{9,8},{10,11... | collective-permute-start | bytes 5505032 | tf_op jit(solution)/shard_map/ppermute | solution.py:44
  86.5 52.9 %copy-start.30 = (bf16[896,512]{1,0:T(8,128)(2,1)}, bf16[896,512]{1,0:T(8,128)(2,1)S(1)}, u32[]{:S(2)}) copy-start(bf16[896,512]{1,0:T(8,128)(2,1)S(1)} %get-tuple-element.63) | copy-start | bytes 2752516
  86.5 52.9 %copy-start.32 = (bf16[896,512]{1,0:T(8,128)(2,1)}, bf16[896,512]{1,0:T(8,128)(2,1)S(1)}, u32[]{:S(2)}) copy-start(bf16[896,512]{1,0:T(8,128)(2,1)S(1)} %get-tuple-element.64) | copy-start | bytes 2752516
  86.8 39.8 %copy-start.9 = (bf16[896,1024]{1,0:T(8,128)(2,1)S(1)}, bf16[896,1024]{1,0:T(8,128)(2,1)}, u32[]{:S(2)}) copy-start(bf16[896,1024]{1,0:T(8,128)(2,1)} %param.16) | copy-start | bytes 5505028
  155.3 42.0 %collective-permute-start.2 = (bf16[896,1024]{1,0:T(8,128)(2,1)}, bf16[896,1024]{1,0:T(8,128)(2,1)}, u32[]{:S(2)}, u32[]{:S(2)}) collective-permute-start(bf16[896,1024]{1,0:T(8,128)(2,1)} %add_convert_fusion.1), channel_id=1, source_target_pairs={{0,1},{1,0},{2,3},{3,2},{4,5},{5,4},{6,7},{7,6},{8,9},{9,8},{10,11... | collective-permute-start | bytes 5505032 | tf_op jit(solution)/shard_map/ppermute | solution.py:44
  160.8 134.7 %collective-permute-start.3 = (bf16[896,512]{1,0:T(8,128)(2,1)}, bf16[896,512]{1,0:T(8,128)(2,1)}, u32[]{:S(2)}, u32[]{:S(2)}) collective-permute-start(bf16[896,512]{1,0:T(8,128)(2,1)} %broadcast_select_fusion.2), channel_id=1, source_target_pairs={{0,1},{1,0},{2,3},{3,2},{4,5},{5,4},{6,7},{7,6},{8,9},{9,8},{10,11... | collective-permute-start | bytes 2752520 | tf_op jit(solution)/shard_map/ppermute | solution.py:44
  227.0 22.4 %all-to-all-start.2 = ((bf16[64,8,432]{2,1,0:T(8,128)(2,1)}), bf16[64,8,432]{2,1,0:T(8,128)(2,1)}, u32[]{:S(2)}, u32[]{:S(2)}) async-start(bf16[64,8,432]{2,1,0:T(8,128)(2,1)} %bitcast.139), calls=%async_computation.2 | async-start | bytes 1048576 | tf_op jit(solution)/shard_map/all_to_all | solution.py:246
  251.9 21.8 %all-to-all-start.3 = ((bf16[64,8,432]{2,1,0:T(8,128)(2,1)}), bf16[64,8,432]{2,1,0:T(8,128)(2,1)}, u32[]{:S(2)}, u32[]{:S(2)}) async-start(bf16[64,8,432]{2,1,0:T(8,128)(2,1)} %copy.85), calls=%async_computation.3 | async-start | bytes 1048576 | tf_op jit(solution)/shard_map/all_to_all | solution.py:250
  273.7 72.7 %all-to-all-start.6 = ((bf16[64,48,864]{2,1,0:T(8,128)(2,1)}), bf16[64,48,864]{2,1,0:T(8,128)(2,1)}, u32[]{:S(2)}, u32[]{:S(2)}) async-start(bf16[64,48,864]{2,1,0:T(8,128)(2,1)} %bitcast.126), calls=%async_computation.6 | async-start | bytes 11010048 | tf_op jit(solution)/shard_map/all_to_all | solution.py:65
  346.4 86.7 %all-to-all-start.5 = ((bf16[64,32,864]{2,1,0:T(8,128)(2,1)}), bf16[64,32,864]{2,1,0:T(8,128)(2,1)}, u32[]{:S(2)}, u32[]{:S(2)}) async-start(bf16[64,32,864]{2,1,0:T(8,128)(2,1)} %bitcast.128), calls=%async_computation.5 | async-start | bytes 7340032 | tf_op jit(solution)/shard_map/all_to_all | solution.py:65
  368.4 49.6 %collective-permute-start.4 = (bf16[896,512]{1,0:T(8,128)(2,1)S(1)}, bf16[896,512]{1,0:T(8,128)(2,1)S(1)}, u32[]{:S(2)}, u32[]{:S(2)}) collective-permute-start(bf16[896,512]{1,0:T(8,128)(2,1)S(1)} %broadcast_select_fusion), channel_id=1, source_target_pairs={{0,1},{1,0},{2,3},{3,2},{4,5},{5,4},{6,7},{7,6},{8,9},{9,8},{10,11... | collective-permute-start | bytes 2752520 | tf_op jit(solution)/shard_map/ppermute | solution.py:44
  371.2 46.9 %copy-start.10 = (f32[896,1024]{1,0:T(8,128)S(1)}, f32[896,1024]{1,0:T(8,128)}, u32[]{:S(2)}) copy-start(f32[896,1024]{1,0:T(8,128)} %get-tuple-element.61) | copy-start | bytes 11010052
  420.3 4.0 collective-permute-start.6
  433.1 63.9 %all-to-all-start.4 = ((bf16[64,16,1920]{2,1,0:T(8,128)(2,1)}), bf16[64,16,1920]{2,1,0:T(8,128)(2,1)}, u32[]{:S(2)}, u32[]{:S(2)}) async-start(bf16[64,16,1920]{2,1,0:T(8,128)(2,1)} %bitcast.127), calls=%async_computation.4 | async-start | bytes 7864320 | tf_op jit(solution)/shard_map/all_to_all | solution.py:65
  443.5 44.2 %copy-start.15 = (f32[896,512]{1,0:T(8,128)S(1)}, f32[896,512]{1,0:T(8,128)}, u32[]{:S(2)}) copy-start(f32[896,512]{1,0:T(8,128)} %get-tuple-element.49) | copy-start | bytes 5505028
  443.5 44.2 %copy-start.82 = (f32[896]{0:T(1024)S(1)}, f32[896]{0:T(1024)}, u32[]{:S(2)}) copy-start(f32[896]{0:T(1024)} %copy-done.81) | copy-start | bytes 10756
  443.5 44.2 %collective-permute-start.5 = (f32[2,896]{1,0:T(2,128)S(1)}, f32[2,896]{1,0:T(2,128)S(1)}, u32[]{:S(2)}, u32[]{:S(2)}) collective-permute-start(f32[2,896]{1,0:T(2,128)S(1)} %pad_maximum_fusion.12), channel_id=1, source_target_pairs={{0,1},{1,0},{2,3},{3,2},{4,5},{5,4},{6,7},{7,6},{8,9},{9,8},{10,11... | collective-permute-start | bytes 21512 | tf_op jit(solution)/shard_map/ppermute | solution.py:44
  446.8 40.9 %copy-start.12 = (f32[896,1024]{1,0:T(8,128)S(1)}, f32[896,1024]{1,0:T(8,128)}, u32[]{:S(2)}) copy-start(f32[896,1024]{1,0:T(8,128)} %copy-done.11) | copy-start | bytes 11010052
  (130 other events, 584.0 us)
